TPU v7x, 256 devices: a whole 4x4x8 slice. The times are simulated.
256 devices in a mesh: inline: 8 (over x, z_lo), xline: 32 (over y, z_hi, core).
Axes of the slice: x: 4, y: 4, z: 8 (z_hi: 4, z_lo: 2; z = z_hi * 2 + z_lo), core: 2. Of those that a mesh axis runs over, the one named last changes fastest.
Arguments:
- traces: float32 [64, 512, 1024], P('inline', 'xline'), may hold values from -6 to 6
- filters: float32 [2, 512, 81], replicated, may hold values from -0.6 to 0.6
Outputs:
- denoised: float32 [64, 512, 1024], P('inline', 'xline')
All inputs are finite; a program needn't handle non-finite values.
Results may differ from a plain program's by a relative error of at most 0.00007.
Values sent between devices are 32-bit elements; how exact they have to be, the bound alone decides.
No kernel may reach another device: no remote copies, remote signals or barrier semaphores. Data moves between devices by JAX's collectives and lax.ppermute only.
A program may use at most 64 MiB of HBM per device.

v0:
```python
import math

import jax
import jax.numpy as jnp
import ml_dtypes
import numpy as np
from jax import lax
from jax.experimental import pallas as pl
from jax.experimental.pallas import tpu as pltpu
from jax.sharding import PartitionSpec as P

ROWS, COLS, NT = 8, 16, 1024
HALF = NT // 2
HALO = 4
TAPS = 9
OUTC = COLS + HALO
FRAME = 32
AXES = ("inline", "xline")


def split_bf16(table):
    high = table.astype(ml_dtypes.bfloat16)
    low = (table - high.astype(np.float64)).astype(ml_dtypes.bfloat16)
    return high, low


def tables():
    time_index = np.arange(HALF)[:, None]
    out = []
    for parity in (0, 1):
        bins = 2 * np.arange(HALF // 2)[None, :] + parity
        phase = (time_index * bins % NT) * (2.0 * math.pi / NT)
        table = np.concatenate([np.cos(phase), -np.sin(phase)], axis=1)
        out.extend(split_bf16(table))
    return np.stack(out)


SUBLANE = ((0, 1, 4, 5), (2, 3, 6, 7))


def high_low(x):
    high = x.astype(jnp.bfloat16)
    return high, (x - high.astype(jnp.float32)).astype(jnp.bfloat16)


def dot3(x, high, low, contract):
    dims = (((1,), (contract,)), ((), ()))
    xh, xl = high_low(x)
    dot = lambda a, b: lax.dot_general(a, b, dims, preferred_element_type=jnp.float32)
    return dot(xh, high) + (dot(xl, high) + dot(xh, low))


def forward(x, tab_ref):
    first, second = x[:, :HALF], x[:, HALF:]
    tiles = [None] * 8
    for parity, value in ((0, first + second), (1, first - second)):
        product = dot3(value, tab_ref[2 * parity], tab_ref[2 * parity + 1], 0)
        for c in range(4):
            tiles[SUBLANE[parity][c]] = product[:, c * 128 : (c + 1) * 128]
    return tiles


def place(tiles, start, count, ref, swapped_ref, base):
    for s in range(8):
        value = tiles[s][start : start + count]
        ref[pl.ds(base * 8 + s, count, stride=8), :] = value
        swapped_ref[pl.ds(base * 8 + (s ^ 4), count, stride=8), :] = value


def filter_row(tap_regs, in_base, out_base, count, ref, swapped_ref, acc_ref):
    acc = [acc_ref[pl.ds((out_base + t) * 8, 8), :] for t in range(count)]
    for e in range(count + TAPS - 1):
        offset = pl.ds((in_base + e) * 8, 8)
        x, xs = ref[offset, :], swapped_ref[offset, :]
        for b in range(TAPS):
            t = e - b
            if 0 <= t < count:
                acc[t] = acc[t] + (tap_regs[b] * x + tap_regs[TAPS + b] * xs)
    for t in range(count):
        acc_ref[pl.ds((out_base + t) * 8, 8), :] = acc[t]


def load_taps(h_ref, a):
    tap = lambda b, part: h_ref[pl.ds(((a * TAPS + b) * 2 + part) * 8, 8), :]
    return [tap(b, 0) for b in range(TAPS)] + [tap(b, 1) for b in range(TAPS)]


def parity_of(axis):
    return lax.rem(lax.axis_index(axis), 2)


def own_kernel(x_ref, side_ref, tab_ref, h_ref, acc_ref, fr, fs, tmp, tmps):
    odd = parity_of("xline")
    column = lax.axis_index("xline")
    is_edge = (column == 0) | (column == lax.axis_size("xline") - 1)
    keep = jnp.where(is_edge, 0.0, 1.0).astype(jnp.float32)
    zero = jnp.zeros((8 * 8, 128), jnp.float32)
    for i in range(ROWS):
        for base in (i * FRAME, i * FRAME + 24):
            fr[pl.ds(base * 8, 64), :] = zero
            fs[pl.ds(base * 8, 64), :] = zero
    tiles = forward(x_ref[...].reshape(ROWS * COLS, NT), tab_ref)
    for i in range(ROWS):
        place(tiles, i * COLS, COLS, fr, fs, i * FRAME + 8)
    side_tiles = forward(side_ref[...], tab_ref)
    place(side_tiles, 0, ROWS * HALO, tmp, tmps, 0)
    side_base = 4 + 20 * odd
    for i in range(ROWS):
        source = pl.ds(i * HALO * 8, HALO * 8)
        target = pl.ds(pl.multiple_of((i * FRAME + side_base) * 8, 8), HALO * 8)
        fr[target, :] = tmp[source, :] * keep
        fs[target, :] = tmps[source, :] * keep
    acc_ref[...] = jnp.zeros_like(acc_ref)
    in_col = HALO - HALO * odd

    def tap_row(a, carry):
        regs = load_taps(h_ref, a)

        def out_row(i, carry):
            for t0 in range(0, OUTC, 10):
                filter_row(regs, (i + a - HALO) * FRAME + in_col + t0, i * OUTC + t0, 10, fr, fs, acc_ref)
            return carry

        return lax.fori_loop(jnp.maximum(0, HALO - a), jnp.minimum(ROWS, ROWS + HALO - a), out_row, carry)

    lax.fori_loop(0, TAPS, tap_row, 0)


def rows_kernel(acc_in, near_ref, far_ref, tab_ref, h_ref, acc_ref, mate_ref, work, fr, fs):
    odd_row, odd = parity_of("inline"), parity_of("xline")
    row = lax.axis_index("inline")
    is_edge = (row == 0) | (row == lax.axis_size("inline") - 1)
    keep = jnp.where(is_edge, 0.0, 1.0).astype(jnp.float32)
    work[...] = acc_in[...]
    zero = jnp.zeros((8 * 8, 128), jnp.float32)
    for i in range(ROWS):
        for base in (i * FRAME, i * FRAME + 24):
            fr[pl.ds(base * 8, 64), :] = zero
            fs[pl.ds(base * 8, 64), :] = zero
    near_tiles = forward(near_ref[...].reshape(HALO * COLS, NT), tab_ref)
    far_tiles = [tile * keep for tile in forward(far_ref[...].reshape(HALO * COLS, NT), tab_ref)]
    is_odd = odd_row == 1
    above = [jnp.where(is_odd, n, f) for n, f in zip(near_tiles, far_tiles)]
    below = [jnp.where(is_odd, f, n) for n, f in zip(near_tiles, far_tiles)]
    for r in range(HALO):
        place(above, r * COLS, COLS, fr, fs, r * FRAME + 8)
        place(below, r * COLS, COLS, fr, fs, (HALO + r) * FRAME + 8)
    in_col = HALO - HALO * odd

    for a in (0, 1, 2, 3, 5, 6, 7, 8):
        regs = load_taps(h_ref, a)

        def out_row(i, carry):
            in_row = i + a if a < HALO else i + a - 2 * HALO
            for t0 in range(0, OUTC, 10):
                filter_row(regs, in_row * FRAME + in_col + t0, i * OUTC + t0, 10, fr, fs, work)
            return carry

        if a < HALO:
            lax.fori_loop(0, HALO - a, out_row, 0)
        else:
            lax.fori_loop(ROWS + HALO - a, ROWS, out_row, 0)
    for i in range(ROWS):
        own = pl.ds(pl.multiple_of((i * OUTC + HALO * odd) * 8, 8), COLS * 8)
        acc_ref[pl.ds(i * COLS * 8, COLS * 8), :] = work[own, :]
        mate = pl.ds(pl.multiple_of((i * OUTC + COLS - COLS * odd) * 8, 8), HALO * 8)
        mate_ref[pl.ds(i * HALO * 8, HALO * 8), :] = work[mate, :]


def last_kernel(acc_in, mate_ref, near_ref, far_ref, tab_ref, h_ref, out_ref, work, fr, fs, tmp, tmps):
    odd_row, odd = parity_of("inline"), parity_of("xline")
    row, column = lax.axis_index("inline"), lax.axis_index("xline")
    row_edge = (row == 0) | (row == lax.axis_size("inline") - 1)
    column_edge = (column == 0) | (column == lax.axis_size("xline") - 1)
    keep_near = jnp.where(column_edge, 0.0, 1.0).astype(jnp.float32)
    keep_far = jnp.where(row_edge, 0.0, keep_near)
    work[...] = acc_in[...]
    fr[...] = jnp.zeros_like(fr)
    fs[...] = jnp.zeros_like(fs)
    corner = jnp.concatenate([near_ref[...], far_ref[...]], axis=0)
    place(forward(corner, tab_ref), 0, 2 * HALO * HALO, tmp, tmps, 0)
    for half, keep in ((0, keep_near), (1, keep_far)):
        first = HALO * (1 - odd_row) if half == 0 else HALO * odd_row
        for r in range(HALO):
            source = pl.ds((half * HALO + r) * HALO * 8, HALO * 8)
            target = pl.ds(pl.multiple_of(((first + r) * 12 + 8 * odd) * 8, 8), HALO * 8)
            fr[target, :] = tmp[source, :] * keep
            fs[target, :] = tmps[source, :] * keep
    out_col = 12 * odd
    for a in (0, 1, 2, 3, 5, 6, 7, 8):
        regs = load_taps(h_ref, a)

        def out_row(i, carry):
            in_row = i + a if a < HALO else i + a - 2 * HALO
            filter_row(regs, in_row * 12, i * COLS + out_col, HALO, fr, fs, work)
            return carry

        if a < HALO:
            lax.fori_loop(0, HALO - a, out_row, 0)
        else:
            lax.fori_loop(ROWS + HALO - a, ROWS, out_row, 0)
    for i in range(ROWS):
        target = pl.ds(pl.multiple_of((i * COLS + 12 - 12 * odd) * 8, 8), HALO * 8)
        work[target, :] = work[target, :] + mate_ref[pl.ds(i * HALO * 8, HALO * 8), :]
    lane = lax.broadcasted_iota(jnp.int32, (ROWS * COLS, 128), 1)
    parts = []
    for parity in (0, 1):
        tiles = [work[pl.ds(s, ROWS * COLS, stride=8), :] for s in SUBLANE[parity]]
        if parity == 0:
            tiles[0] = jnp.where(lane == 0, 0.5 * tiles[0], tiles[0])
        spectrum = jnp.concatenate(tiles, axis=1)
        parts.append(dot3(spectrum, tab_ref[2 * parity], tab_ref[2 * parity + 1], 1) * (2.0 / NT))
    out_ref[:, :, :HALF] = (parts[0] + parts[1]).reshape(ROWS, COLS, HALF)
    out_ref[:, :, HALF:] = (parts[0] - parts[1]).reshape(ROWS, COLS, HALF)


def call(kernel, outs, scratch, args):
    return pl.pallas_call(
        kernel,
        out_shape=[jax.ShapeDtypeStruct(shape, jnp.float32) for shape in outs],
        scratch_shapes=[pltpu.VMEM(shape, jnp.float32) for shape in scratch],
        compiler_params=pltpu.CompilerParams(vmem_limit_bytes=40 * 2**20),
    )(*args)


def permutations(inline, xline):
    number = lambda i, j: i * xline + j
    side, far = [], []
    for i in range(inline):
        for j in range(xline):
            k = j - 1 if j % 2 == 0 else j + 1
            side.append((number(i, j), number(i, k) if 0 <= k < xline else number(i ^ 1, j)))
            k = i - 1 if i % 2 == 0 else i + 1
            far.append((number(i, j), number(k, j) if 0 <= k < inline else number(i, j ^ 1)))
    near = [(i, i ^ 1) for i in range(inline)]
    mate = [(j, j ^ 1) for j in range(xline)]
    return side, far, near, mate


def per_device(traces, filters):
    side, far, near, mate = permutations(lax.axis_size("inline"), lax.axis_size("xline"))
    odd_row, odd = parity_of("inline"), parity_of("xline")
    tab = jnp.asarray(tables())

    edge = lax.dynamic_slice_in_dim(traces, 12 * odd, HALO, 1).reshape(ROWS * HALO, NT)
    edge, traces = lax.optimization_barrier((edge, traces))
    from_side = lax.ppermute(edge, AXES, side)
    to_near = lax.dynamic_slice_in_dim(traces, HALO - HALO * odd_row, HALO, 0)
    to_far = lax.dynamic_slice_in_dim(traces, HALO * odd_row, HALO, 0)
    from_far = lax.ppermute(to_far, AXES, far)
    from_near = lax.ppermute(to_near, "inline", near)
    corner = HALO * HALO
    corner_far = lax.ppermute(lax.dynamic_slice_in_dim(from_side, corner * odd_row, corner, 0), AXES, far)
    corner_near = lax.ppermute(lax.dynamic_slice_in_dim(from_side, corner - corner * odd_row, corner, 0), "inline", near)

    h = jnp.transpose(filters.reshape(2, HALF // 2, 2, TAPS * TAPS), (0, 3, 2, 1)).reshape(2, TAPS * TAPS, 4, 128)
    h = jnp.stack([jnp.concatenate([h[0], h[0]], 1), jnp.concatenate([-h[1], h[1]], 1)], 1)
    h = h.reshape(TAPS * TAPS * 16, 128)

    frame = (ROWS * FRAME * 8, 128)
    spot = (ROWS * HALO * 8, 128)
    (acc,) = call(own_kernel, [(ROWS * OUTC * 8, 128)], [frame, frame, spot, spot], (traces, from_side, tab, h))
    acc, to_mate = call(
        rows_kernel,
        [(ROWS * COLS * 8, 128), spot],
        [(ROWS * OUTC * 8, 128), frame, frame],
        (acc, from_near, from_far, tab, h),
    )
    from_mate = lax.ppermute(to_mate, "xline", mate)
    corner_frame = (ROWS * 12 * 8, 128)
    (out,) = call(
        last_kernel,
        [(ROWS, COLS, NT)],
        [(ROWS * COLS * 8, 128), corner_frame, corner_frame, spot, spot],
        (acc, from_mate, corner_near, corner_far, tab, h),
    )
    return out


def solution(mesh):
    return jax.shard_map(
        per_device,
        mesh=mesh,
        in_specs=(P("inline", "xline", None), P()),
        out_specs=P("inline", "xline", None),
        check_vma=False,
    )
```

profile of v0, /device:TPU:24, one launch (start us, length us, event | category | flops | bytes accessed | tf_op | source)
XLA Modules:
  0.0 39.2 jit_solution(3870284365340943974)
XLA Ops:
  0.0 1.0 %constant_dynamic-slice_fusion.4 = f32[8,4,1024]{2,1,0:T(4,128)S(1)} fusion(f32[8,16,1024]{2,1,0:T(8,128)} %x_ref, s32[]{:T(128)S(6)} %select_n.15), kind=kLoop, calls=%fused_computation.7 | loop fusion | bytes 262148 | tf_op jit(solution)/shard_map/dynamic_slice | solution.py:245
  1.0 6.0 %collective-permute-start = (f32[32,1024]{1,0:T(8,128)S(1)}, f32[32,1024]{1,0:T(8,128)S(1)}, u32[]{:S(2)}, u32[]{:S(2)}) collective-permute-start(f32[32,1024]{1,0:T(8,128)S(1)} %reshape.14), channel_id=1, source_target_pairs={{0,32},{1,2},{2,1},{3,4},{4,3},{5,6},{6,5},{7,8},{8,7},{9,10},{10,... | collective-permute-start | bytes 393224 | tf_op jit(solution)/shard_map/ppermute | solution.py:247
  7.0 1.9 %constant_dynamic-slice_fusion.2 = (f32[4,16,1024]{2,1,0:T(8,128)}, f32[4,16,1024]{2,1,0:T(8,128)}) fusion(f32[8,16,1024]{2,1,0:T(8,128)} %x_ref, s32[]{:T(128)S(6)} %select_n.17, s32[]{:T(128)S(6)} %select_n.16), kind=kLoop, calls=%fused_computation.5 | loop fusion | bytes 1048584 | tf_op jit(solution)/shard_map/dynamic_slice | solution.py:249
  8.9 0.0 collective-permute-start.2
  8.9 3.0 %collective-permute-start.1 = (f32[4,16,1024]{2,1,0:T(8,128)}, f32[4,16,1024]{2,1,0:T(8,128)}, u32[]{:S(2)}, u32[]{:S(2)}) collective-permute-start(f32[4,16,1024]{2,1,0:T(8,128)} %get-tuple-element.14), channel_id=1, source_target_pairs={{0,32},{32,0},{64,96},{96,64},{128,160},{160,128},{192,224},{224,1... | collective-permute-start | bytes 786440 | tf_op jit(solution)/shard_map/ppermute | solution.py:251
  11.9 1.2 %copy.7 = f32[2,512,81]{2,1,0:T(8,128)S(1)} copy(f32[2,512,81]{1,0,2:T(2,128)} %param.4) | data formatting | bytes 663552 | tf_op args[1]
  13.1 0.1 copy.8
  13.3 0.8 %squeeze.8 = f32[81,4,128]{2,1,0:T(4,128)} reshape(f32[1,81,2,256]{3,2,1,0:T(2,128)S(1)} %copy.8) | data formatting | bytes 331776 | tf_op jit(solution)/shard_map/squeeze | solution.py:257
  14.1 0.1 copy.9
  14.3 0.2 squeeze.9
  14.4 0.0 copy-start
  14.4 0.0 copy-start.1
  14.5 2.0 %maximum_bitcast_fusion = (f32[81,1,8,128]{3,2,0,1:T(8,128)S(1)}, f32[81,1,8,128]{3,2,0,1:T(8,128)}) fusion(f32[81,4,128]{2,1,0:T(4,128)} %squeeze.8, f32[81,4,128]{2,1,0:T(4,128)S(1)} %squeeze.9, f32[81,4,128]{2,1,0:T(4,128)S(1)} %neg.3), kind=kLoop, calls=%fused_computation.1 | loop fusion | flops 165888 | bytes 1161216 | tf_op jit(solution)/shard_map/stack | solution.py:257
  16.5 1.0 %pad_maximum_fusion = f32[81,2,8,128]{3,2,0,1:T(8,128)S(1)} fusion(f32[81,1,8,128]{3,2,0,1:T(8,128)} %get-tuple-element.20, f32[81,1,8,128]{3,2,0,1:T(8,128)S(1)} %get-tuple-element.19), kind=kLoop, calls=%fused_computation | loop fusion | flops 165888 | bytes 1327104 | tf_op jit(solution)/shard_map/stack | solution.py:257
  17.6 0.0 collective-permute-done.side_ref
  17.6 0.0 copy-done
  17.6 0.0 copy-done.1
  17.6 6.8 %shard_map.37.acc_in = f32[1280,128]{1,0:T(8,128)S(1)} custom-call(f32[8,16,1024]{2,1,0:T(8,128)S(1)} %copy-done.1, f32[32,1024]{1,0:T(8,128)S(1)} %collective-permute-done.side_ref, bf16[4,512,512]{2,1,0:T(8,128)(2,1)S(1)} %copy-done, f32[1296,128]{1,0:T(8,128)S(1)} %bitcast.8), custom_call_target="tpu_custom_call" | custom-call | tf_op jit(solution)/shard_map/pallas_call | solution.py:218
  24.4 0.0 collective-permute-done.2.far_ref
  24.4 0.0 collective-permute-done.1.near_ref
  24.4 4.5 %shard_map.38 = (f32[1024,128]{1,0:T(8,128)S(1)}, f32[256,128]{1,0:T(8,128)S(1)}) custom-call(f32[1280,128]{1,0:T(8,128)S(1)} %shard_map.37.acc_in, f32[4,16,1024]{2,1,0:T(8,128)} %collective-permute-done.1.near_ref, f32[4,16,1024]{2,1,0:T(8,128)} %collective-permute-done.2.far_ref, bf16[4,512,512]{2,1,0:T(8,128)(2,1)S(1)} %copy-done, f32[1296,128]{1,0:T(8,128)S(1)} %bitcast.9), custom_call_target="tpu_custom_call" | custom-call | tf_op jit(solution)/shard_map/pallas_call | solution.py:218
  29.0 0.1 collective-permute-start.3
  29.1 0.6 %collective-permute-start.5 = (f32[16,1024]{1,0:T(8,128)S(1)}, f32[16,1024]{1,0:T(8,128)S(1)}, u32[]{:S(2)}, u32[]{:S(2)}) collective-permute-start(f32[16,1024]{1,0:T(8,128)S(1)} %get-tuple-element.17), channel_id=1, source_target_pairs={{0,1},{1,0},{2,3},{3,2},{4,5},{5,4},{6,7},{7,6},{8,9},{9,8},{10,11... | collective-permute-start | bytes 196616 | tf_op jit(solution)/shard_map/ppermute | solution.py:253
  29.7 2.5 %collective-permute-start.4 = (f32[16,1024]{1,0:T(8,128)S(1)}, f32[16,1024]{1,0:T(8,128)S(1)}, u32[]{:S(2)}, u32[]{:S(2)}) collective-permute-start(f32[16,1024]{1,0:T(8,128)S(1)} %get-tuple-element.18), channel_id=1, source_target_pairs={{0,32},{32,0},{64,96},{96,64},{128,160},{160,128},{192,224},{224,1... | collective-permute-start | bytes 196616 | tf_op jit(solution)/shard_map/ppermute | solution.py:254
  32.1 0.0 collective-permute-done.5.far_ref
  32.1 3.9 %collective-permute-done.4.near_ref = f32[16,1024]{1,0:T(8,128)S(1)} collective-permute-done((f32[16,1024]{1,0:T(8,128)S(1)}, f32[16,1024]{1,0:T(8,128)S(1)}, u32[]{:S(2)}, u32[]{:S(2)}) %collective-permute-start.4) | collective-permute-done | bytes 65568 | tf_op jit(solution)/shard_map/ppermute | solution.py:254
  36.0 0.0 collective-permute-done.3.mate_ref
  36.0 3.2 %shard_map.39 = f32[8,16,1024]{2,1,0:T(8,128)} custom-call(f32[1024,128]{1,0:T(8,128)S(1)} %get-tuple-element.11.acc_in, f32[256,128]{1,0:T(8,128)S(1)} %collective-permute-done.3.mate_ref, f32[16,1024]{1,0:T(8,128)S(1)} %collective-permute-done.4.near_ref, f32[16,1024]{1,0:T(8,128)S(1)} %collective-permute-done.5.far_ref, bf16[4,512,512]{2,1,0:T(8,128)(2,1)S(1)} %copy-done, ...), custom_call_target="tpu_custom_call" | custom-call | tf_op jit(solution)/shard_map/pallas_call | solution.py:218
  (5 shorter events, 0.2 us)
Async XLA Ops:
  1.0 16.6 %collective-permute-start = (f32[32,1024]{1,0:T(8,128)S(1)}, f32[32,1024]{1,0:T(8,128)S(1)}, u32[]{:S(2)}, u32[]{:S(2)}) collective-permute-start(f32[32,1024]{1,0:T(8,128)S(1)} %reshape.14), channel_id=1, source_target_pairs={{0,32},{1,2},{2,1},{3,4},{4,3},{5,6},{6,5},{7,8},{8,7},{9,10},{10,... | collective-permute-start | bytes 393224 | tf_op jit(solution)/shard_map/ppermute | solution.py:247
  8.9 15.5 %collective-permute-start.2 = (f32[4,16,1024]{2,1,0:T(8,128)}, f32[4,16,1024]{2,1,0:T(8,128)}, u32[]{:S(2)}, u32[]{:S(2)}) collective-permute-start(f32[4,16,1024]{2,1,0:T(8,128)} %get-tuple-element.13), channel_id=1, source_target_pairs={{0,1},{1,0},{2,3},{3,2},{4,5},{5,4},{6,7},{7,6},{8,9},{9,8},{10,11... | collective-permute-start | bytes 786440 | tf_op jit(solution)/shard_map/ppermute | solution.py:250
  8.9 15.5 %collective-permute-start.1 = (f32[4,16,1024]{2,1,0:T(8,128)}, f32[4,16,1024]{2,1,0:T(8,128)}, u32[]{:S(2)}, u32[]{:S(2)}) collective-permute-start(f32[4,16,1024]{2,1,0:T(8,128)} %get-tuple-element.14), channel_id=1, source_target_pairs={{0,32},{32,0},{64,96},{96,64},{128,160},{160,128},{192,224},{224,1... | collective-permute-start | bytes 786440 | tf_op jit(solution)/shard_map/ppermute | solution.py:251
  14.4 3.2 %copy-start = (bf16[4,512,512]{2,1,0:T(8,128)(2,1)S(1)}, bf16[4,512,512]{2,1,0:T(8,128)(2,1)}, u32[]{:S(2)}) copy-start(bf16[4,512,512]{2,1,0:T(8,128)(2,1)} %constant.32.clone.tab_ref) | copy-start | bytes 6291460
  14.4 3.2 %copy-start.1 = (f32[8,16,1024]{2,1,0:T(8,128)S(1)}, f32[8,16,1024]{2,1,0:T(8,128)}, u32[]{:S(2)}) copy-start(f32[8,16,1024]{2,1,0:T(8,128)} %x_ref) | copy-start | bytes 1572868
  29.0 7.0 %collective-permute-start.3 = (f32[256,128]{1,0:T(8,128)S(1)}, f32[256,128]{1,0:T(8,128)S(1)}, u32[]{:S(2)}, u32[]{:S(2)}) collective-permute-start(f32[256,128]{1,0:T(8,128)S(1)} %get-tuple-element.12), channel_id=1, source_target_pairs={{0,1},{1,0},{2,3},{3,2},{4,5},{5,4},{6,7},{7,6},{8,9},{9,8},{10,11... | collective-permute-start | bytes 393224 | tf_op jit(solution)/shard_map/ppermute | solution.py:269
  29.1 3.0 %collective-permute-start.5 = (f32[16,1024]{1,0:T(8,128)S(1)}, f32[16,1024]{1,0:T(8,128)S(1)}, u32[]{:S(2)}, u32[]{:S(2)}) collective-permute-start(f32[16,1024]{1,0:T(8,128)S(1)} %get-tuple-element.17), channel_id=1, source_target_pairs={{0,1},{1,0},{2,3},{3,2},{4,5},{5,4},{6,7},{7,6},{8,9},{9,8},{10,11... | collective-permute-start | bytes 196616 | tf_op jit(solution)/shard_map/ppermute | solution.py:253
  29.7 6.3 %collective-permute-start.4 = (f32[16,1024]{1,0:T(8,128)S(1)}, f32[16,1024]{1,0:T(8,128)S(1)}, u32[]{:S(2)}, u32[]{:S(2)}) collective-permute-start(f32[16,1024]{1,0:T(8,128)S(1)} %get-tuple-element.18), channel_id=1, source_target_pairs={{0,32},{32,0},{64,96},{96,64},{128,160},{160,128},{192,224},{224,1... | collective-permute-start | bytes 196616 | tf_op jit(solution)/shard_map/ppermute | solution.py:254
where the time goes:
time: 39.4 us; the launch traced here: 39.2 us
  Pallas kernels  14.5 us (37%)
  starting transfers between devices  12.1 us (31%)
  local copies, waits for them, and re-layouts  5.51 us (14%)
  waiting for transfers between devices  3.87 us (10%)
  other arithmetic  3.06 us (8%)
    pallas_call x3, Pallas kernels, call(): pl.pallas_call(kernel, out_shape=[jax.ShapeDtypeStruct(shape, jnp.float32...  14.5 us
    ppermute x1, starting transfers between devices, per_device(): from_side = lax.ppermute(edge, AXES, side)  6.01 us
    ppermute x1, waiting for transfers between devices, per_device(): lax.ppermute(lax.dynamic_slice_in_dim(from_side, corner - corner * odd_ro...  3.85 us
    another operation x2, other arithmetic, per_device(): jnp.stack([jnp.concatenate([h[0], h[0]], 1), jnp.concatenate([-h[1], h[1]...  3.02 us
    ppermute x1, starting transfers between devices, per_device(): from_near = lax.ppermute(to_near, 'inline', near)  2.95 us
    ppermute x1, starting transfers between devices, per_device(): lax.ppermute(lax.dynamic_slice_in_dim(from_side, corner - corner * odd_ro...  2.47 us
    dynamic_slice x1, local copies, waits for them, and re-layouts, per_device(): to_far = lax.dynamic_slice_in_dim(traces, HALO * odd_row, HALO, 0)  1.88 us
    unnamed x5, local copies, waits for them, and re-layouts  1.2 us
  transfers between devices with their start and end apart: 6, of which 1 were waited for; matrix products, arithmetic and copies ran while one was open for 19% of the time, Pallas kernels for 17%

commit v1 on v0

v1 whole, which is shorter than its diff:
```python
import math

import jax
import jax.numpy as jnp
import ml_dtypes
import numpy as np
from jax import lax
from jax.experimental import pallas as pl
from jax.experimental.pallas import tpu as pltpu
from jax.sharding import PartitionSpec as P

ROWS, COLS, NT = 8, 16, 1024
HALF = NT // 2
HALO = 4
TAPS = 9
WIDE = COLS + HALO
AXES = ("inline", "xline")
OUTER_ROWS = (0, 1, 2, 3, 5, 6, 7, 8)


def split_bf16(table):
    high = table.astype(ml_dtypes.bfloat16)
    low = (table - high.astype(np.float64)).astype(ml_dtypes.bfloat16)
    return high, low


def tables():
    time_index = np.arange(HALF)[:, None]
    out = []
    for parity in (0, 1):
        bins = 2 * np.arange(HALF // 2)[None, :] + parity
        phase = (time_index * bins % NT) * (2.0 * math.pi / NT)
        table = np.concatenate([np.cos(phase), -np.sin(phase)], axis=1)
        out.extend(split_bf16(table))
    return np.stack(out)


def bin_order():
    order = np.concatenate([np.arange(0, HALF, 2), np.arange(1, HALF, 2)])
    return (np.arange(HALF)[:, None] == order[None, :]).astype(ml_dtypes.bfloat16)


SUBLANE = ((0, 1, 4, 5), (2, 3, 6, 7))


def dot(a, b, contract=0):
    return lax.dot_general(a, b, (((1,), (contract,)), ((), ())), preferred_element_type=jnp.float32)


def high_low(x):
    high = x.astype(jnp.bfloat16)
    return high, (x - high.astype(jnp.float32)).astype(jnp.bfloat16)


def dot3(x, high, low, contract):
    xh, xl = high_low(x)
    return dot(xh, high, contract) + (dot(xl, high, contract) + dot(xh, low, contract))


def forward(x, tab_ref):
    first, second = x[:, :HALF], x[:, HALF:]
    tiles = [None] * 8
    for parity, value in ((0, first + second), (1, first - second)):
        product = dot3(value, tab_ref[2 * parity], tab_ref[2 * parity + 1], 0)
        for c in range(4):
            tiles[SUBLANE[parity][c]] = product[:, c * 128 : (c + 1) * 128]
    return tiles


def place(tiles, start, count, ref, swapped_ref, base):
    for s in range(8):
        value = tiles[s][start : start + count]
        ref[pl.ds(base * 8 + s, count, stride=8), :] = value
        swapped_ref[pl.ds(base * 8 + (s ^ 4), count, stride=8), :] = value


def filter_row(regs, ref, swapped_ref, in_base, inputs, acc_ref, out_base, outputs, shift):
    spot = lambda base, n: pl.ds((base + n) * 8, 8)
    acc = {t: acc_ref[spot(out_base, t), :] for t in outputs}
    for n in inputs:
        pairs = [(n - b + shift, b) for b in range(TAPS) if n - b + shift in acc]
        if pairs:
            x, xs = ref[spot(in_base, n - inputs[0]), :], swapped_ref[spot(in_base, n - inputs[0]), :]
            for t, b in pairs:
                acc[t] = acc[t] + (regs[b] * x + regs[TAPS + b] * xs)
    for t in outputs:
        acc_ref[spot(out_base, t), :] = acc[t]


def load_taps(h_ref, a):
    tap = lambda b, part: h_ref[pl.ds(((a * TAPS + b) * 2 + part) * 8, 8), :]
    return [tap(b, 0) for b in range(TAPS)] + [tap(b, 1) for b in range(TAPS)]


def parity_of(axis):
    return lax.rem(lax.axis_index(axis), 2)


def keep_of(axis):
    index = lax.axis_index(axis)
    is_end = (index == 0) | (index == lax.axis_size(axis) - 1)
    return jnp.where(is_end, 0.0, 1.0).astype(jnp.float32)


def each_parity(body):
    odd = parity_of("xline")
    for parity in (0, 1):
        pl.when(odd == parity)(lambda: body(parity))


def edges_kernel(x_ref, edge_ref, far_ref, near_ref):
    odd_row = parity_of("inline")

    def body(parity):
        first = 12 * parity
        for i in range(ROWS):
            row = lax.rem(i + HALO * odd_row, ROWS)
            edge_ref[i * HALO : (i + 1) * HALO, :] = x_ref[row, first : first + HALO, :]

    each_parity(body)
    for r in range(HALO):
        far_ref[r * COLS : (r + 1) * COLS, :] = x_ref[HALO * odd_row + r]
        near_ref[r * COLS : (r + 1) * COLS, :] = x_ref[HALO - HALO * odd_row + r]


def taps_kernel(f_ref, order_ref, x_ref, tab_ref, h_ref):
    rest, taps = f_ref[...], 0.0
    for _ in range(3):
        part = rest.astype(jnp.bfloat16)
        rest = rest - part.astype(jnp.float32)
        taps = taps + dot(part, order_ref[...])
    count = 2 * TAPS * TAPS
    is_imag = lax.rem(lax.broadcasted_iota(jnp.int32, (count, 128), 0), 2) == 1
    for s in range(4):
        value = taps[:, s * 128 : (s + 1) * 128]
        h_ref[pl.ds(s, count, stride=8), :] = jnp.where(is_imag, -value, value)
        h_ref[pl.ds(s + 4, count, stride=8), :] = value


def corners_kernel(side_ref, h_ref, far_ref, near_ref):
    far_ref[...] = side_ref[: HALO * HALO, :]
    near_ref[...] = side_ref[HALO * HALO :, :]


def own_kernel(x_ref, side_ref, tab_ref, h_ref, acc_ref, fr, fs, tmp, tmps):
    odd_row = parity_of("inline")
    keep = keep_of("xline")
    tiles = forward(x_ref[...].reshape(ROWS * COLS, NT), tab_ref)
    place(forward(side_ref[...], tab_ref), 0, ROWS * HALO, tmp, tmps, 0)
    acc_ref[...] = jnp.zeros_like(acc_ref)

    def body(parity):
        side_first = COLS * parity
        for i in range(ROWS):
            place(tiles, i * COLS, COLS, fr, fs, i * WIDE + HALO - HALO * parity)
            row = lax.rem(i + HALO * odd_row, ROWS)
            source = pl.ds(i * HALO * 8, HALO * 8)
            target = pl.ds(pl.multiple_of((row * WIDE + side_first) * 8, 8), HALO * 8)
            fr[target, :] = tmp[source, :] * keep
            fs[target, :] = tmps[source, :] * keep

        def tap_row(a, carry):
            regs = load_taps(h_ref, a)

            def out_row(i, carry):
                for t0 in (0, WIDE // 2):
                    outputs = range(t0, t0 + WIDE // 2)
                    filter_row(
                        regs, fr, fs, (i + a - HALO) * WIDE, range(WIDE), acc_ref, i * WIDE, outputs, 8 * parity
                    )
                return carry

            return lax.fori_loop(jnp.maximum(0, HALO - a), jnp.minimum(ROWS, ROWS + HALO - a), out_row, carry)

        lax.fori_loop(0, TAPS, tap_row, 0)

    each_parity(body)


def outer_rows(h_ref, body):
    for a in OUTER_ROWS:
        regs = load_taps(h_ref, a)
        above = a < HALO

        def out_row(i, carry):
            body(regs, i + a if above else i + a - 2 * HALO, i)
            return carry

        lax.fori_loop(0 if above else ROWS + HALO - a, HALO - a if above else ROWS, out_row, 0)


def rows_kernel(acc_ref, near_ref, far_ref, tab_ref, h_ref, mate_ref, fr, fs):
    odd_row = parity_of("inline")
    keep = keep_of("inline")
    near_tiles = forward(near_ref[...], tab_ref)
    far_tiles = [tile * keep for tile in forward(far_ref[...], tab_ref)]
    is_odd = odd_row == 1
    above = [jnp.where(is_odd, n, f) for n, f in zip(near_tiles, far_tiles)]
    below = [jnp.where(is_odd, f, n) for n, f in zip(near_tiles, far_tiles)]
    place(above, 0, HALO * COLS, fr, fs, 0)
    place(below, 0, HALO * COLS, fr, fs, HALO * COLS)

    def body(parity):
        first = COLS - COLS * parity
        for i in range(ROWS):
            mate_ref[pl.ds(i * HALO * 8, HALO * 8), :] = acc_ref[pl.ds((i * WIDE + first) * 8, HALO * 8), :]
        inputs = range(COLS, WIDE) if parity == 0 else range(0, HALO)
        skip = COLS - HALO if parity == 0 else 0
        shift = 8 * parity - first

        def filter_out(regs, frame_row, i):
            filter_row(
                regs, fr, fs, frame_row * COLS + skip, inputs, mate_ref, i * HALO, range(HALO), shift
            )

        outer_rows(h_ref, filter_out)

    each_parity(body)


def inner_kernel(acc_ref, fr, fs, near_ref, far_ref, tab_ref, h_ref, out_ref, cr, cs, tmp, tmps):
    odd_row = parity_of("inline")
    keep_near = keep_of("xline")
    keep_far = keep_near * keep_of("inline")
    corner = jnp.concatenate([near_ref[...], far_ref[...]], axis=0)
    place(forward(corner, tab_ref), 0, 2 * HALO * HALO, tmp, tmps, 0)
    size = HALO * HALO * 8
    for half, keep in ((0, keep_near), (1, keep_far)):
        first = 1 - odd_row if half == 0 else odd_row
        source, target = pl.ds(half * size, size), pl.ds(pl.multiple_of(first * size, 8), size)
        cr[target, :] = tmp[source, :] * keep
        cs[target, :] = tmps[source, :] * keep

    def body(parity):
        own = HALO * parity
        for i in range(ROWS):
            out_ref[pl.ds(i * COLS * 8, COLS * 8), :] = acc_ref[pl.ds((i * WIDE + own) * 8, COLS * 8), :]
        inputs = range(HALO - own, WIDE - own)
        side = range(0, HALO) if parity == 0 else range(COLS, WIDE)
        near_side = range(0, HALO) if parity == 0 else range(COLS - HALO, COLS)
        shift = 8 * parity - own

        def filter_out(regs, frame_row, i):
            for t0 in (0, COLS // 2):
                filter_row(
                    regs, fr, fs, frame_row * COLS, inputs, out_ref, i * COLS, range(t0, t0 + COLS // 2), shift
                )
            filter_row(regs, cr, cs, frame_row * HALO, side, out_ref, i * COLS, near_side, shift)

        outer_rows(h_ref, filter_out)

    each_parity(body)


def inverse_kernel(acc_ref, mate_ref, tab_ref, out_ref, work):
    odd = parity_of("xline")
    work[...] = acc_ref[...]
    for i in range(ROWS):
        target = pl.ds(pl.multiple_of((i * COLS + 12 - 12 * odd) * 8, 8), HALO * 8)
        work[target, :] = work[target, :] + mate_ref[pl.ds(i * HALO * 8, HALO * 8), :]
    lane = lax.broadcasted_iota(jnp.int32, (ROWS * COLS, 128), 1)
    parts = []
    for parity in (0, 1):
        tiles = [work[pl.ds(s, ROWS * COLS, stride=8), :] for s in SUBLANE[parity]]
        if parity == 0:
            tiles[0] = jnp.where(lane == 0, 0.5 * tiles[0], tiles[0])
        spectrum = jnp.concatenate(tiles, axis=1)
        parts.append(dot3(spectrum, tab_ref[2 * parity], tab_ref[2 * parity + 1], 1) * (2.0 / NT))
    out_ref[:, :, :HALF] = (parts[0] + parts[1]).reshape(ROWS, COLS, HALF)
    out_ref[:, :, HALF:] = (parts[0] - parts[1]).reshape(ROWS, COLS, HALF)


def call(kernel, outs, scratch, args, specs=None, weight=0):
    return pl.pallas_call(
        kernel,
        out_shape=[jax.ShapeDtypeStruct(shape, jnp.float32) for shape in outs],
        in_specs=specs or [pl.BlockSpec()] * len(args),
        scratch_shapes=[pltpu.VMEM(shape, jnp.float32) for shape in scratch],
        compiler_params=pltpu.CompilerParams(vmem_limit_bytes=40 * 2**20),
        cost_estimate=pl.CostEstimate(flops=weight * 10**9, bytes_accessed=0, transcendentals=0) if weight else None,
    )(*args)


def permutations(inline, xline):
    number = lambda i, j: i * xline + j
    side, far = [], []
    for i in range(inline):
        for j in range(xline):
            k = j - 1 if j % 2 == 0 else j + 1
            side.append((number(i, j), number(i, k) if 0 <= k < xline else number(i ^ 1, j)))
            k = i - 1 if i % 2 == 0 else i + 1
            far.append((number(i, j), number(k, j) if 0 <= k < inline else number(i, j ^ 1)))
    near = [(i, i ^ 1) for i in range(inline)]
    mate = [(j, j ^ 1) for j in range(xline)]
    return side, far, near, mate


def per_device(traces, filters):
    side, far, near, mate = permutations(lax.axis_size("inline"), lax.axis_size("xline"))
    tab = jnp.asarray(tables())
    taps = jnp.transpose(filters, (2, 0, 1)).reshape(2 * TAPS * TAPS, HALF)

    rows = (HALO * COLS, NT)
    corner = HALO * HALO
    edge, to_far, to_near = call(edges_kernel, [(ROWS * HALO, NT), rows, rows], [], (traces,))
    from_side = lax.ppermute(edge, AXES, side)
    from_far = lax.ppermute(to_far, AXES, far)
    from_near = lax.ppermute(to_near, "inline", near)
    vmem, anywhere = pl.BlockSpec(memory_space=pltpu.VMEM), pl.BlockSpec(memory_space=pl.ANY)
    (h,) = call(
        taps_kernel, [(2 * TAPS * TAPS * 8, 128)], [], (taps, jnp.asarray(bin_order()), traces, tab), weight=1
    )
    for_far, for_near = call(corners_kernel, [(corner, NT)] * 2, [], (from_side, h), [vmem, anywhere])
    corner_far = lax.ppermute(for_far, AXES, far)
    corner_near = lax.ppermute(for_near, "inline", near)

    wide = (ROWS * WIDE * 8, 128)
    frame = (ROWS * COLS * 8, 128)
    spot = (ROWS * HALO * 8, 128)
    (acc,) = call(own_kernel, [wide], [wide, wide, spot, spot], (traces, from_side, tab, h), weight=10)
    to_mate, fr, fs = call(rows_kernel, [spot, frame, frame], [], (acc, from_near, from_far, tab, h))
    from_mate = lax.ppermute(to_mate, "xline", mate)
    (acc,) = call(inner_kernel, [frame], [spot] * 4, (acc, fr, fs, corner_near, corner_far, tab, h), weight=10)
    (out,) = call(inverse_kernel, [(ROWS, COLS, NT)], [frame], (acc, from_mate, tab))
    return out


def solution(mesh):
    return jax.shard_map(
        per_device,
        mesh=mesh,
        in_specs=(P("inline", "xline", None), P()),
        out_specs=P("inline", "xline", None),
        check_vma=False,
    )
```

time: 39.4 us -> 30.1 us (0.76)
  the two profiles are of different devices: /device:TPU:24 before, /device:TPU:57 now
where the time goes in v1:
time: 30.1 us; the launch traced here: 29.8 us
  Pallas kernels  12.1 us (40%)
  starting transfers between devices  11.7 us (39%)
  local copies, waits for them, and re-layouts  5.92 us (20%)
    pallas_call x7, Pallas kernels, call(): pl.pallas_call(kernel, out_shape=[jax.ShapeDtypeStruct(shape, jnp.float32...  12.1 us
    unnamed x10, local copies, waits for them, and re-layouts  4.71 us
    ppermute x1, starting transfers between devices, per_device(): from_side = lax.ppermute(edge, AXES, side)  3.65 us
    ppermute x1, starting transfers between devices, per_device(): from_mate = lax.ppermute(to_mate, 'xline', mate)  3.18 us
    ppermute x1, starting transfers between devices, per_device(): from_far = lax.ppermute(to_far, AXES, far)  2.39 us
    ppermute x1, starting transfers between devices, per_device(): corner_near = lax.ppermute(for_near, 'inline', near)  1.58 us
    reshape x1, local copies, waits for them, and re-layouts, per_device(): taps = jnp.transpose(filters, (2, 0, 1)).reshape(2 * TAPS * TAPS, HALF)  1.2 us
    ppermute x1, starting transfers between devices, per_device(): corner_far = lax.ppermute(for_far, AXES, far)  0.9 us
  transfers between devices with their start and end apart: 6, of which 0 were waited for; matrix products, arithmetic and copies ran while one was open for 4% of the time, Pallas kernels for 34%

profile of v1, /device:TPU:57, one launch (start us, length us, event | category | flops | bytes accessed | tf_op | source)
XLA Modules:
  0.0 29.8 jit_solution(16280157280272150299)
XLA Ops:
  0.0 0.0 copy-start.2
  0.0 1.0 %copy-done.2 = f32[8,16,1024]{2,1,0:T(8,128)S(1)} copy-done((f32[8,16,1024]{2,1,0:T(8,128)S(1)}, f32[8,16,1024]{2,1,0:T(8,128)}, u32[]{:S(2)}) %copy-start.2) | copy-done | bytes 524312
  1.0 0.1 shard_map.46
  1.1 3.6 %collective-permute-start = (f32[32,1024]{1,0:T(8,128)S(1)}, f32[32,1024]{1,0:T(8,128)S(1)}, u32[]{:S(2)}, u32[]{:S(2)}) collective-permute-start(f32[32,1024]{1,0:T(8,128)S(1)} %get-tuple-element.13), channel_id=1, source_target_pairs={{0,32},{1,2},{2,1},{3,4},{4,3},{5,6},{6,5},{7,8},{8,7},{9,10},{10,... | collective-permute-start | bytes 393224 | tf_op jit(solution)/shard_map/ppermute | solution.py:306
  4.8 0.0 collective-permute-start.1
  4.8 2.4 %collective-permute-start.2 = (f32[64,1024]{1,0:T(8,128)S(1)}, f32[64,1024]{1,0:T(8,128)S(1)}, u32[]{:S(2)}, u32[]{:S(2)}) collective-permute-start(f32[64,1024]{1,0:T(8,128)S(1)} %get-tuple-element.15), channel_id=1, source_target_pairs={{0,1},{1,0},{2,3},{3,2},{4,5},{5,4},{6,7},{7,6},{8,9},{9,8},{10,11... | collective-permute-start | bytes 786440 | tf_op jit(solution)/shard_map/ppermute | solution.py:307
  7.2 1.2 %reshape.3.f_ref = f32[162,512]{1,0:T(8,128)S(1)} reshape(f32[81,2,512]{2,1,0:T(2,128)} %bitcast.1) | data formatting | bytes 663552 | tf_op jit(solution)/shard_map/reshape | solution.py:301
  8.4 0.0 copy-start
  8.4 1.6 %copy-done = bf16[4,512,512]{2,1,0:T(8,128)(2,1)S(1)} copy-done((bf16[4,512,512]{2,1,0:T(8,128)(2,1)S(1)}, bf16[4,512,512]{2,1,0:T(8,128)(2,1)}, u32[]{:S(2)}) %copy-start) | copy-done | bytes 2097176
  10.0 0.0 copy-start.3
  10.0 1.0 %copy-done.3 = f32[8,16,1024]{2,1,0:T(8,128)S(1)} copy-done((f32[8,16,1024]{2,1,0:T(8,128)S(1)}, f32[8,16,1024]{2,1,0:T(8,128)}, u32[]{:S(2)}) %copy-start.3) | copy-done | bytes 524312
  11.0 0.0 copy-start.4
  11.0 1.0 %copy-done.4 = bf16[512,512]{1,0:T(8,128)(2,1)S(1)} copy-done((bf16[512,512]{1,0:T(8,128)(2,1)S(1)}, bf16[512,512]{1,0:T(8,128)(2,1)}, u32[]{:S(2)}) %copy-start.4) | copy-done | bytes 524312
  12.0 0.0 copy-start.1
  12.0 0.5 %shard_map.47.h_ref = f32[1296,128]{1,0:T(8,128)S(1)} custom-call(f32[162,512]{1,0:T(8,128)S(1)} %reshape.3.f_ref, bf16[512,512]{1,0:T(8,128)(2,1)S(1)} %copy-done.4, f32[8,16,1024]{2,1,0:T(8,128)S(1)} %copy-done.3, bf16[4,512,512]{2,1,0:T(8,128)(2,1)S(1)} %copy-done), custom_call_target="tpu_custom_call" | custom-call | flops 1000000000 | tf_op jit(solution)/shard_map/pallas_call | solution.py:274
  12.6 0.0 collective-permute-done.side_ref
  12.6 1.6 %collective-permute-start.3 = (f32[16,1024]{1,0:T(8,128)S(1)}, f32[16,1024]{1,0:T(8,128)S(1)}, u32[]{:S(2)}, u32[]{:S(2)}) collective-permute-start(f32[16,1024]{1,0:T(8,128)S(1)} %get-tuple-element.18), channel_id=1, source_target_pairs={{0,32},{32,0},{64,96},{96,64},{128,160},{160,128},{192,224},{224,1... | collective-permute-start | bytes 196616 | tf_op jit(solution)/shard_map/ppermute | solution.py:315
  14.2 0.9 %collective-permute-start.4 = (f32[16,1024]{1,0:T(8,128)S(1)}, f32[16,1024]{1,0:T(8,128)S(1)}, u32[]{:S(2)}, u32[]{:S(2)}) collective-permute-start(f32[16,1024]{1,0:T(8,128)S(1)} %get-tuple-element.19), channel_id=1, source_target_pairs={{0,1},{1,0},{2,3},{3,2},{4,5},{5,4},{6,7},{7,6},{8,9},{9,8},{10,11... | collective-permute-start | bytes 196616 | tf_op jit(solution)/shard_map/ppermute | solution.py:314
  15.1 0.0 copy-done.1
  15.1 5.7 %shard_map.48.acc_ref = f32[1280,128]{1,0:T(8,128)S(1)} custom-call(f32[8,16,1024]{2,1,0:T(8,128)S(1)} %copy-done.3, f32[32,1024]{1,0:T(8,128)S(1)} %collective-permute-done.side_ref, bf16[4,512,512]{2,1,0:T(8,128)(2,1)S(1)} %copy-done.1, f32[1296,128]{1,0:T(8,128)S(1)} %shard_map.47.h_ref), custom_call_target="tpu_custom_call" | custom-call | flops 10000000000 | tf_op jit(solution)/shard_map/pallas_call | solution.py:274
  20.8 0.0 collective-permute-done.1.near_ref
  20.8 0.0 collective-permute-done.2.far_ref
  20.8 1.5 %shard_map.49 = (f32[256,128]{1,0:T(8,128)S(1)}, f32[1024,128]{1,0:T(8,128)S(1)}, f32[1024,128]{1,0:T(8,128)S(1)}) custom-call(f32[1280,128]{1,0:T(8,128)S(1)} %shard_map.48.acc_ref, f32[64,1024]{1,0:T(8,128)S(1)} %collective-permute-done.1.near_ref, f32[64,1024]{1,0:T(8,128)S(1)} %collective-permute-done.2.far_ref, bf16[4,512,512]{2,1,0:T(8,128)(2,1)S(1)} %copy-done.1, ...), custom_call_target="tpu_custom_call" | custom-call | tf_op jit(solution)/shard_map/pallas_call | solution.py:274
  22.4 3.2 %collective-permute-start.5 = (f32[256,128]{1,0:T(8,128)S(1)}, f32[256,128]{1,0:T(8,128)S(1)}, u32[]{:S(2)}, u32[]{:S(2)}) collective-permute-start(f32[256,128]{1,0:T(8,128)S(1)} %get-tuple-element.20), channel_id=1, source_target_pairs={{0,1},{1,0},{2,3},{3,2},{4,5},{5,4},{6,7},{7,6},{8,9},{9,8},{10,11... | collective-permute-start | bytes 393224 | tf_op jit(solution)/shard_map/ppermute | solution.py:322
  25.6 0.0 collective-permute-done.3.near_ref
  25.6 0.0 collective-permute-done.4.far_ref
  25.6 2.2 %shard_map.51.acc_ref = f32[1024,128]{1,0:T(8,128)S(1)} custom-call(f32[1280,128]{1,0:T(8,128)S(1)} %shard_map.48.acc_ref, f32[1024,128]{1,0:T(8,128)S(1)} %get-tuple-element.16.fr, f32[1024,128]{1,0:T(8,128)S(1)} %get-tuple-element.17.fs, f32[16,1024]{1,0:T(8,128)S(1)} %collective-permute-done.3.near_ref, f32[16,1024]{1,0:T(8,128)S(1)} %collective-permute-done.4.far_ref, ...), custom_call_target="tpu_custom_call" | custom-call | flops 10000000000 | tf_op jit(solution)/shard_map/pallas_call | solution.py:274
  27.8 0.0 collective-permute-done.5.mate_ref
  27.8 2.0 %shard_map.52 = f32[8,16,1024]{2,1,0:T(8,128)} custom-call(f32[1024,128]{1,0:T(8,128)S(1)} %shard_map.51.acc_ref, f32[256,128]{1,0:T(8,128)S(1)} %collective-permute-done.5.mate_ref, bf16[4,512,512]{2,1,0:T(8,128)(2,1)S(1)} %copy-done.1), custom_call_target="tpu_custom_call" | custom-call | tf_op jit(solution)/shard_map/pallas_call | solution.py:274
  (1 shorter events, 0.0 us)
Async XLA Ops:
  0.0 1.0 %copy-start.2 = (f32[8,16,1024]{2,1,0:T(8,128)S(1)}, f32[8,16,1024]{2,1,0:T(8,128)}, u32[]{:S(2)}) copy-start(f32[8,16,1024]{2,1,0:T(8,128)} %x_ref.5) | copy-start | bytes 1572868
  1.1 11.4 %collective-permute-start = (f32[32,1024]{1,0:T(8,128)S(1)}, f32[32,1024]{1,0:T(8,128)S(1)}, u32[]{:S(2)}, u32[]{:S(2)}) collective-permute-start(f32[32,1024]{1,0:T(8,128)S(1)} %get-tuple-element.13), channel_id=1, source_target_pairs={{0,32},{1,2},{2,1},{3,4},{4,3},{5,6},{6,5},{7,8},{8,7},{9,10},{10,... | collective-permute-start | bytes 393224 | tf_op jit(solution)/shard_map/ppermute | solution.py:306
  4.8 16.1 %collective-permute-start.1 = (f32[64,1024]{1,0:T(8,128)S(1)}, f32[64,1024]{1,0:T(8,128)S(1)}, u32[]{:S(2)}, u32[]{:S(2)}) collective-permute-start(f32[64,1024]{1,0:T(8,128)S(1)} %get-tuple-element.14), channel_id=1, source_target_pairs={{0,32},{32,0},{64,96},{96,64},{128,160},{160,128},{192,224},{224,1... | collective-permute-start | bytes 786440 | tf_op jit(solution)/shard_map/ppermute | solution.py:308
  4.8 16.1 %collective-permute-start.2 = (f32[64,1024]{1,0:T(8,128)S(1)}, f32[64,1024]{1,0:T(8,128)S(1)}, u32[]{:S(2)}, u32[]{:S(2)}) collective-permute-start(f32[64,1024]{1,0:T(8,128)S(1)} %get-tuple-element.15), channel_id=1, source_target_pairs={{0,1},{1,0},{2,3},{3,2},{4,5},{5,4},{6,7},{7,6},{8,9},{9,8},{10,11... | collective-permute-start | bytes 786440 | tf_op jit(solution)/shard_map/ppermute | solution.py:307
  8.4 1.6 %copy-start = (bf16[4,512,512]{2,1,0:T(8,128)(2,1)S(1)}, bf16[4,512,512]{2,1,0:T(8,128)(2,1)}, u32[]{:S(2)}) copy-start(bf16[4,512,512]{2,1,0:T(8,128)(2,1)} %constant.4.clone.tab_ref) | copy-start | bytes 6291460
  10.0 1.0 %copy-start.3 = (f32[8,16,1024]{2,1,0:T(8,128)S(1)}, f32[8,16,1024]{2,1,0:T(8,128)}, u32[]{:S(2)}) copy-start(f32[8,16,1024]{2,1,0:T(8,128)} %x_ref.5) | copy-start | bytes 1572868
  11.0 1.0 %copy-start.4 = (bf16[512,512]{1,0:T(8,128)(2,1)S(1)}, bf16[512,512]{1,0:T(8,128)(2,1)}, u32[]{:S(2)}) copy-start(bf16[512,512]{1,0:T(8,128)(2,1)} %constant.5.clone.order_ref) | copy-start | bytes 1572868
  12.0 3.0 %copy-start.1 = (bf16[4,512,512]{2,1,0:T(8,128)(2,1)S(1)}, bf16[4,512,512]{2,1,0:T(8,128)(2,1)}, u32[]{:S(2)}) copy-start(bf16[4,512,512]{2,1,0:T(8,128)(2,1)} %constant.4.clone.tab_ref) | copy-start | bytes 6291460
  12.6 13.0 %collective-permute-start.3 = (f32[16,1024]{1,0:T(8,128)S(1)}, f32[16,1024]{1,0:T(8,128)S(1)}, u32[]{:S(2)}, u32[]{:S(2)}) collective-permute-start(f32[16,1024]{1,0:T(8,128)S(1)} %get-tuple-element.18), channel_id=1, source_target_pairs={{0,32},{32,0},{64,96},{96,64},{128,160},{160,128},{192,224},{224,1... | collective-permute-start | bytes 196616 | tf_op jit(solution)/shard_map/ppermute | solution.py:315
  14.2 11.4 %collective-permute-start.4 = (f32[16,1024]{1,0:T(8,128)S(1)}, f32[16,1024]{1,0:T(8,128)S(1)}, u32[]{:S(2)}, u32[]{:S(2)}) collective-permute-start(f32[16,1024]{1,0:T(8,128)S(1)} %get-tuple-element.19), channel_id=1, source_target_pairs={{0,1},{1,0},{2,3},{3,2},{4,5},{5,4},{6,7},{7,6},{8,9},{9,8},{10,11... | collective-permute-start | bytes 196616 | tf_op jit(solution)/shard_map/ppermute | solution.py:314
  22.4 5.4 %collective-permute-start.5 = (f32[256,128]{1,0:T(8,128)S(1)}, f32[256,128]{1,0:T(8,128)S(1)}, u32[]{:S(2)}, u32[]{:S(2)}) collective-permute-start(f32[256,128]{1,0:T(8,128)S(1)} %get-tuple-element.20), channel_id=1, source_target_pairs={{0,1},{1,0},{2,3},{3,2},{4,5},{5,4},{6,7},{7,6},{8,9},{9,8},{10,11... | collective-permute-start | bytes 393224 | tf_op jit(solution)/shard_map/ppermute | solution.py:322

commit v2 on v1

v2 whole, which is shorter than its diff:
```python
import math

import jax
import jax.numpy as jnp
import ml_dtypes
import numpy as np
from jax import lax
from jax.experimental import pallas as pl
from jax.experimental.pallas import tpu as pltpu
from jax.sharding import PartitionSpec as P

ROWS, COLS, NT = 8, 16, 1024
HALF = NT // 2
HALO = 4
TAPS = 9
WIDE = COLS + 2 * HALO
CHUNK = 12
AXES = ("inline", "xline")


def split_bf16(table):
    high = table.astype(ml_dtypes.bfloat16)
    low = (table - high.astype(np.float64)).astype(ml_dtypes.bfloat16)
    return high, low


def tables():
    time_index = np.arange(HALF)[:, None]
    out, transposed = [], []
    for parity in (0, 1):
        bins = 2 * np.arange(HALF // 2)[None, :] + parity
        phase = (time_index * bins % NT) * (2.0 * math.pi / NT)
        table = np.concatenate([np.cos(phase), -np.sin(phase)], axis=1)
        out.extend(split_bf16(table))
        transposed.extend(split_bf16(table.T))
    return np.stack(out), np.stack(transposed)


SUBLANE = ((0, 1, 4, 5), (2, 3, 6, 7))


def dot(a, b):
    return lax.dot_general(a, b, (((1,), (0,)), ((), ())), preferred_element_type=jnp.float32)


def high_low(x):
    high = x.astype(jnp.bfloat16)
    return high, (x - high.astype(jnp.float32)).astype(jnp.bfloat16)


def dot3(x, high, low):
    xh, xl = high_low(x)
    return dot(xh, high) + (dot(xl, high) + dot(xh, low))


def forward(x, tab_ref):
    first, second = x[:, :HALF], x[:, HALF:]
    tiles = [None] * 8
    for parity, value in ((0, first + second), (1, first - second)):
        product = dot3(value, tab_ref[2 * parity], tab_ref[2 * parity + 1])
        for c in range(4):
            tiles[SUBLANE[parity][c]] = product[:, c * 128 : (c + 1) * 128]
    return tiles


def place(tiles, start, count, ref, swapped_ref, base):
    for s in range(8):
        value = tiles[s][start : start + count]
        ref[pl.ds(base * 8 + s, count, stride=8), :] = value
        swapped_ref[pl.ds(base * 8 + (s ^ 4), count, stride=8), :] = value


def filter_row(regs, ref, swapped_ref, in_base, inputs, acc_ref, out_base, outputs):
    spot = lambda base, n: pl.ds((base + n) * 8, 8)
    acc = {t: acc_ref[spot(out_base, t), :] for t in outputs}
    for n in inputs:
        pairs = [(n - b + 2 * HALO, b) for b in range(TAPS) if n - b + 2 * HALO in acc]
        if pairs:
            x, xs = ref[spot(in_base, n), :], swapped_ref[spot(in_base, n), :]
            for t, b in pairs:
                acc[t] = acc[t] + (regs[b] * x + regs[TAPS + b] * xs)
    for t in outputs:
        acc_ref[spot(out_base, t), :] = acc[t]


def load_taps(h_ref, a):
    tap = lambda b, part: h_ref[pl.ds(((a * TAPS + b) * 2 + part) * 8, 8), :]
    return [tap(b, 0) for b in range(TAPS)] + [tap(b, 1) for b in range(TAPS)]


def parity_of(axis):
    return lax.rem(lax.axis_index(axis), 2)


def keep_of(axis):
    index = lax.axis_index(axis)
    is_end = (index == 0) | (index == lax.axis_size(axis) - 1)
    return jnp.where(is_end, 0.0, 1.0).astype(jnp.float32)


def edges_kernel(x_ref, far_ref, near_ref):
    odd_row = parity_of("inline")
    for r in range(HALO):
        far_ref[r * COLS : (r + 1) * COLS, :] = x_ref[HALO * odd_row + r]
        near_ref[r * COLS : (r + 1) * COLS, :] = x_ref[HALO - HALO * odd_row + r]


def taps_kernel(f_ref, h_ref):
    source = lax.broadcasted_iota(jnp.int32, (HALF, HALF), 0)
    target = lax.broadcasted_iota(jnp.int32, (HALF, HALF), 1)
    wanted = jnp.where(target < HALF // 2, 2 * target, 2 * target - (HALF - 1))
    order = jnp.where(source == wanted, 1.0, 0.0).astype(jnp.bfloat16)
    count = TAPS * TAPS
    for part in (0, 1):
        rest = jnp.concatenate([f_ref[pl.ds(2 * tile + part, count, stride=8), :] for tile in range(4)], axis=1)
        taps = 0.0
        for _ in range(3):
            piece = rest.astype(jnp.bfloat16)
            rest = rest - piece.astype(jnp.float32)
            taps = taps + dot(piece, order)
        for s in range(4):
            value = taps[:, s * 128 : (s + 1) * 128]
            h_ref[pl.ds(part * 8 + s, count, stride=16), :] = -value if part else value
            h_ref[pl.ds(part * 8 + s + 4, count, stride=16), :] = value


def filter_columns(regs, fr, fs, row, acc_ref, i):
    for t0 in range(0, WIDE, CHUNK):
        filter_row(regs, fr, fs, row * COLS, range(COLS), acc_ref, i * WIDE, range(t0, t0 + CHUNK))


def own_kernel(x_ref, tab_ref, h_ref, acc_ref, fr, fs):
    place(forward(x_ref[...].reshape(ROWS * COLS, NT), tab_ref), 0, ROWS * COLS, fr, fs, 0)
    acc_ref[...] = jnp.zeros_like(acc_ref)

    def tap_row(a, carry):
        regs = load_taps(h_ref, a)

        def out_row(i, carry):
            filter_columns(regs, fr, fs, i + a - HALO, acc_ref, i)
            return carry

        return lax.fori_loop(jnp.maximum(0, HALO - a), jnp.minimum(ROWS, ROWS + HALO - a), out_row, carry)

    lax.fori_loop(0, TAPS, tap_row, 0)


def neighbour_rows(h_ref, below, body):
    for step in range(HALO):
        regs = load_taps(h_ref, step + (HALO + 1) * below)

        def out_row(i, carry):
            body(regs, i + step - 7 * below, i)
            return carry

        first = (ROWS - 1 - step) * below
        lax.fori_loop(first, HALO - step + (HALO + step) * below, out_row, 0)


def near_kernel(acc_in, near_ref, tab_ref, h_ref, acc_ref, fr, fs):
    acc_ref[...] = acc_in[...]
    place(forward(near_ref[...], tab_ref), 0, HALO * COLS, fr, fs, 0)
    neighbour_rows(
        h_ref, 1 - parity_of("inline"), lambda regs, row, i: filter_columns(regs, fr, fs, row, acc_ref, i)
    )


def ends_kernel(acc_ref, far_ref, tab_ref, h_ref, side_ref, mate_ref, fr, fs):
    keep = keep_of("inline")
    tiles = [tile * keep for tile in forward(far_ref[...], tab_ref)]
    place(tiles, 0, HALO * COLS, fr, fs, 0)

    def body(parity):
        left_ref, right_ref = (side_ref, mate_ref) if parity == 0 else (mate_ref, side_ref)
        right = WIDE - HALO
        for i in range(ROWS):
            target = pl.ds(i * HALO * 8, HALO * 8)
            left_ref[target, :] = acc_ref[pl.ds(i * WIDE * 8, HALO * 8), :]
            right_ref[target, :] = acc_ref[pl.ds((i * WIDE + right) * 8, HALO * 8), :]

        def far_out(regs, row, i):
            base = row * COLS
            filter_row(regs, fr, fs, base, range(HALO), left_ref, i * HALO, range(HALO))
            filter_row(
                regs, fr, fs, base, range(COLS - HALO, COLS), right_ref, i * HALO - right, range(right, WIDE)
            )

        neighbour_rows(h_ref, parity_of("inline"), far_out)

    odd = parity_of("xline")
    for parity in (0, 1):
        pl.when(odd == parity)(lambda: body(parity))


def inner_kernel(acc_ref, fr, fs, h_ref, out_ref):
    for i in range(ROWS):
        out_ref[pl.ds(i * COLS * 8, COLS * 8), :] = acc_ref[pl.ds((i * WIDE + HALO) * 8, COLS * 8), :]

    def far_out(regs, row, i):
        for t0 in (HALO, HALO + COLS // 2):
            outputs = range(t0, t0 + COLS // 2)
            filter_row(regs, fr, fs, row * COLS, range(COLS), out_ref, i * COLS - HALO, outputs)

    neighbour_rows(h_ref, parity_of("inline"), far_out)


def inverse_kernel(acc_ref, side_ref, mate_ref, tab_ref, out_ref, work):
    odd = parity_of("xline")
    keep = keep_of("xline")
    work[...] = acc_ref[...]
    for i in range(ROWS):
        source = pl.ds(i * HALO * 8, HALO * 8)
        side = pl.ds(pl.multiple_of((i * COLS + 12 * odd) * 8, 8), HALO * 8)
        work[side, :] = work[side, :] + side_ref[source, :] * keep
        mate = pl.ds(pl.multiple_of((i * COLS + 12 - 12 * odd) * 8, 8), HALO * 8)
        work[mate, :] = work[mate, :] + mate_ref[source, :]
    lane = lax.broadcasted_iota(jnp.int32, (ROWS * COLS, 128), 1)
    parts = []
    for parity in (0, 1):
        tiles = [work[pl.ds(s, ROWS * COLS, stride=8), :] for s in SUBLANE[parity]]
        if parity == 0:
            tiles[0] = jnp.where(lane == 0, 0.5 * tiles[0], tiles[0])
        spectrum = jnp.concatenate(tiles, axis=1)
        parts.append(dot3(spectrum, tab_ref[2 * parity], tab_ref[2 * parity + 1]) * (2.0 / NT))
    out_ref[:, :, :HALF] = (parts[0] + parts[1]).reshape(ROWS, COLS, HALF)
    out_ref[:, :, HALF:] = (parts[0] - parts[1]).reshape(ROWS, COLS, HALF)


def call(kernel, outs, scratch, args, weight=0):
    return pl.pallas_call(
        kernel,
        out_shape=[jax.ShapeDtypeStruct(shape, jnp.float32) for shape in outs],
        scratch_shapes=[pltpu.VMEM(shape, jnp.float32) for shape in scratch],
        compiler_params=pltpu.CompilerParams(vmem_limit_bytes=40 * 2**20),
        cost_estimate=pl.CostEstimate(flops=weight * 10**9, bytes_accessed=0, transcendentals=0) if weight else None,
    )(*args)


def permutations(inline, xline):
    number = lambda i, j: i * xline + j
    side, far = [], []
    for i in range(inline):
        for j in range(xline):
            k = j - 1 if j % 2 == 0 else j + 1
            side.append((number(i, j), number(i, k) if 0 <= k < xline else number(i ^ 1, j)))
            k = i - 1 if i % 2 == 0 else i + 1
            far.append((number(i, j), number(k, j) if 0 <= k < inline else number(i, j ^ 1)))
    near = [(i, i ^ 1) for i in range(inline)]
    mate = [(j, j ^ 1) for j in range(xline)]
    return side, far, near, mate


def per_device(traces, filters):
    side, far, near, mate = permutations(lax.axis_size("inline"), lax.axis_size("xline"))
    tab, inverse_tab = (jnp.asarray(table) for table in tables())
    taps = jnp.transpose(filters.reshape(2, HALF // 128, 128, TAPS * TAPS), (3, 1, 0, 2)).reshape(-1, 128)

    rows = (HALO * COLS, NT)
    to_far, to_near = call(edges_kernel, [rows, rows], [], (traces,), weight=2)
    from_far = lax.ppermute(to_far, AXES, far)
    from_near = lax.ppermute(to_near, "inline", near)

    wide = (ROWS * WIDE * 8, 128)
    frame = (ROWS * COLS * 8, 128)
    spot = (ROWS * HALO * 8, 128)
    rows_frame = (HALO * COLS * 8, 128)
    (h,) = call(taps_kernel, [(2 * TAPS * TAPS * 8, 128)], [], (taps,), weight=1)
    (acc,) = call(own_kernel, [wide], [frame, frame], (traces, tab, h), weight=10)
    (acc,) = call(near_kernel, [wide], [rows_frame] * 2, (acc, from_near, tab, h), weight=2)
    to_side, to_mate, fr, fs = call(ends_kernel, [spot, spot, rows_frame, rows_frame], [], (acc, from_far, tab, h))
    from_mate = lax.ppermute(to_mate, "xline", mate)
    from_side = lax.ppermute(to_side, AXES, side)
    (acc,) = call(inner_kernel, [frame], [], (acc, fr, fs, h), weight=2)
    (out,) = call(inverse_kernel, [(ROWS, COLS, NT)], [frame], (acc, from_side, from_mate, inverse_tab))
    return out


def solution(mesh):
    return jax.shard_map(
        per_device,
        mesh=mesh,
        in_specs=(P("inline", "xline", None), P()),
        out_specs=P("inline", "xline", None),
        check_vma=False,
    )
```

time: 30.1 us -> 26.8 us (0.89)
  the two profiles are of different devices: /device:TPU:57 before, /device:TPU:30 now
where the time goes in v2:
time: 26.8 us; the launch traced here: 26.6 us
  Pallas kernels  10.5 us (39%)
  waiting for transfers between devices  7.61 us (28%)
  starting transfers between devices  7.34 us (27%)
  local copies, waits for them, and re-layouts  1.06 us (4%)
    pallas_call x7, Pallas kernels, call(): pl.pallas_call(kernel, out_shape=[jax.ShapeDtypeStruct(shape, jnp.float32...  10.5 us
    ppermute x1, starting transfers between devices, per_device(): from_side = lax.ppermute(to_side, AXES, side)  4.96 us
    ppermute x1, waiting for transfers between devices, per_device(): from_far = lax.ppermute(to_far, AXES, far)  3.9 us
    ppermute x1, waiting for transfers between devices, per_device(): from_side = lax.ppermute(to_side, AXES, side)  3.2 us
    ppermute x1, starting transfers between devices, per_device(): from_near = lax.ppermute(to_near, 'inline', near)  2 us
    unnamed x10, local copies, waits for them, and re-layouts  1.06 us
  transfers between devices with their start and end apart: 4, of which 3 were waited for; matrix products, arithmetic and copies ran while one was open for 0% of the time, Pallas kernels for 31%

profile of v2, /device:TPU:30, one launch (start us, length us, event | category | flops | bytes accessed | tf_op | source)
XLA Modules:
  0.0 26.6 jit_solution(3836378796706008072)
XLA Ops:
  0.0 0.0 copy-start.2
  0.0 1.0 %copy-done.2 = f32[8,16,1024]{2,1,0:T(8,128)S(1)} copy-done((f32[8,16,1024]{2,1,0:T(8,128)S(1)}, f32[8,16,1024]{2,1,0:T(8,128)}, u32[]{:S(2)}) %copy-start.2) | copy-done | bytes 524312
  1.0 0.0 copy-start.4
  1.1 0.0 copy-start
  1.1 0.0 copy-start.3
  1.1 2.0 %collective-permute-start = (f32[64,1024]{1,0:T(8,128)S(1)}, f32[64,1024]{1,0:T(8,128)S(1)}, u32[]{:S(2)}, u32[]{:S(2)}) collective-permute-start(f32[64,1024]{1,0:T(8,128)S(1)} %get-tuple-element.11), channel_id=1, source_target_pairs={{0,32},{32,0},{64,96},{96,64},{128,160},{160,128},{192,224},{224,1... | collective-permute-start | bytes 786440 | tf_op jit(solution)/shard_map/ppermute | solution.py:261
  3.1 0.4 %collective-permute-start.1 = (f32[64,1024]{1,0:T(8,128)S(1)}, f32[64,1024]{1,0:T(8,128)S(1)}, u32[]{:S(2)}, u32[]{:S(2)}) collective-permute-start(f32[64,1024]{1,0:T(8,128)S(1)} %get-tuple-element.12), channel_id=1, source_target_pairs={{0,1},{1,0},{2,3},{3,2},{4,5},{5,4},{6,7},{7,6},{8,9},{9,8},{10,11... | collective-permute-start | bytes 786440 | tf_op jit(solution)/shard_map/ppermute | solution.py:260
  3.5 0.0 copy-done.4
  3.5 0.8 %shard_map.46.h_ref = f32[1296,128]{1,0:T(8,128)S(1)} custom-call(f32[648,128]{1,0:T(8,128)S(1)} %bitcast.5), custom_call_target="tpu_custom_call" | custom-call | flops 1000000000 | tf_op jit(solution)/shard_map/pallas_call | solution.py:230
  4.3 0.0 copy-done
  4.3 0.0 copy-done.3
  4.3 5.0 %shard_map.47.acc_in = f32[1536,128]{1,0:T(8,128)S(1)} custom-call(f32[8,16,1024]{2,1,0:T(8,128)S(1)} %copy-done.3, bf16[4,512,512]{2,1,0:T(8,128)(2,1)S(1)} %copy-done, f32[1296,128]{1,0:T(8,128)S(1)} %shard_map.46.h_ref), custom_call_target="tpu_custom_call" | custom-call | flops 10000000000 | tf_op jit(solution)/shard_map/pallas_call | solution.py:230
  9.3 0.5 %collective-permute-done.near_ref = f32[64,1024]{1,0:T(8,128)S(1)} collective-permute-done((f32[64,1024]{1,0:T(8,128)S(1)}, f32[64,1024]{1,0:T(8,128)S(1)}, u32[]{:S(2)}, u32[]{:S(2)}) %collective-permute-start) | collective-permute-done | bytes 262176 | tf_op jit(solution)/shard_map/ppermute | solution.py:261
  9.8 1.6 %shard_map.49.acc_ref = f32[1536,128]{1,0:T(8,128)S(1)} custom-call(f32[1536,128]{1,0:T(8,128)S(1)} %shard_map.47.acc_in, f32[64,1024]{1,0:T(8,128)S(1)} %collective-permute-done.near_ref, bf16[4,512,512]{2,1,0:T(8,128)(2,1)S(1)} %copy-done, f32[1296,128]{1,0:T(8,128)S(1)} %shard_map.46.h_ref), custom_call_target="tpu_custom_call" | custom-call | flops 2000000000 | tf_op jit(solution)/shard_map/pallas_call | solution.py:230
  11.4 3.9 %collective-permute-done.1.far_ref = f32[64,1024]{1,0:T(8,128)S(1)} collective-permute-done((f32[64,1024]{1,0:T(8,128)S(1)}, f32[64,1024]{1,0:T(8,128)S(1)}, u32[]{:S(2)}, u32[]{:S(2)}) %collective-permute-start.1) | collective-permute-done | bytes 262176 | tf_op jit(solution)/shard_map/ppermute | solution.py:260
  15.3 0.9 %shard_map.50 = (f32[256,128]{1,0:T(8,128)S(1)}, f32[256,128]{1,0:T(8,128)S(1)}, f32[512,128]{1,0:T(8,128)S(1)}, f32[512,128]{1,0:T(8,128)S(1)}) custom-call(f32[1536,128]{1,0:T(8,128)S(1)} %shard_map.49.acc_ref, f32[64,1024]{1,0:T(8,128)S(1)} %collective-permute-done.1.far_ref, bf16[4,512,512]{2,1,0:T(8,128)(2,1)S(1)} %copy-done, ...), custom_call_target="tpu_custom_call" | custom-call | tf_op jit(solution)/shard_map/pallas_call | solution.py:230
  16.2 5.0 %collective-permute-start.2 = (f32[256,128]{1,0:T(8,128)S(1)}, f32[256,128]{1,0:T(8,128)S(1)}, u32[]{:S(2)}, u32[]{:S(2)}) collective-permute-start(f32[256,128]{1,0:T(8,128)S(1)} %get-tuple-element.15), channel_id=1, source_target_pairs={{0,32},{1,2},{2,1},{3,4},{4,3},{5,6},{6,5},{7,8},{8,7},{9,10},{10,... | collective-permute-start | bytes 393224 | tf_op jit(solution)/shard_map/ppermute | solution.py:272
  21.2 0.0 collective-permute-start.3
  21.2 0.0 copy-start.1
  21.2 0.8 %shard_map.51.acc_ref = f32[1024,128]{1,0:T(8,128)S(1)} custom-call(f32[1536,128]{1,0:T(8,128)S(1)} %shard_map.49.acc_ref, f32[512,128]{1,0:T(8,128)S(1)} %get-tuple-element.13.fr, f32[512,128]{1,0:T(8,128)S(1)} %get-tuple-element.14.fs, f32[1296,128]{1,0:T(8,128)S(1)} %shard_map.46.h_ref), custom_call_target="tpu_custom_call" | custom-call | flops 2000000000 | tf_op jit(solution)/shard_map/pallas_call | solution.py:230
  22.0 3.2 %collective-permute-done.2.side_ref = f32[256,128]{1,0:T(8,128)S(1)} collective-permute-done((f32[256,128]{1,0:T(8,128)S(1)}, f32[256,128]{1,0:T(8,128)S(1)}, u32[]{:S(2)}, u32[]{:S(2)}) %collective-permute-start.2) | collective-permute-done | bytes 131104 | tf_op jit(solution)/shard_map/ppermute | solution.py:272
  25.2 0.0 collective-permute-done.3.mate_ref
  25.2 0.0 copy-done.1
  25.2 1.5 %shard_map.52 = f32[8,16,1024]{2,1,0:T(8,128)} custom-call(f32[1024,128]{1,0:T(8,128)S(1)} %shard_map.51.acc_ref, f32[256,128]{1,0:T(8,128)S(1)} %collective-permute-done.2.side_ref, f32[256,128]{1,0:T(8,128)S(1)} %collective-permute-done.3.mate_ref, bf16[4,512,512]{2,1,0:T(8,128)(2,1)S(1)} %copy-done.1), custom_call_target="tpu_custom_call" | custom-call | tf_op jit(solution)/shard_map/pallas_call | solution.py:230
  (1 shorter events, 0.0 us)
Async XLA Ops:
  0.0 1.0 %copy-start.2 = (f32[8,16,1024]{2,1,0:T(8,128)S(1)}, f32[8,16,1024]{2,1,0:T(8,128)}, u32[]{:S(2)}) copy-start(f32[8,16,1024]{2,1,0:T(8,128)} %x_ref.3) | copy-start | bytes 1572868
  1.0 2.4 %copy-start.4 = (f32[2,512,81]{1,0,2:T(2,128)S(1)}, f32[2,512,81]{1,0,2:T(2,128)}, u32[]{:S(2)}) copy-start(f32[2,512,81]{1,0,2:T(2,128)} %param.5) | copy-start | bytes 995332
  1.1 3.2 %copy-start = (bf16[4,512,512]{2,1,0:T(8,128)(2,1)S(1)}, bf16[4,512,512]{2,1,0:T(8,128)(2,1)}, u32[]{:S(2)}) copy-start(bf16[4,512,512]{2,1,0:T(8,128)(2,1)} %constant.4.clone.tab_ref) | copy-start | bytes 6291460
  1.1 3.2 %copy-start.3 = (f32[8,16,1024]{2,1,0:T(8,128)S(1)}, f32[8,16,1024]{2,1,0:T(8,128)}, u32[]{:S(2)}) copy-start(f32[8,16,1024]{2,1,0:T(8,128)} %x_ref.3) | copy-start | bytes 1572868
  1.1 8.7 %collective-permute-start = (f32[64,1024]{1,0:T(8,128)S(1)}, f32[64,1024]{1,0:T(8,128)S(1)}, u32[]{:S(2)}, u32[]{:S(2)}) collective-permute-start(f32[64,1024]{1,0:T(8,128)S(1)} %get-tuple-element.11), channel_id=1, source_target_pairs={{0,32},{32,0},{64,96},{96,64},{128,160},{160,128},{192,224},{224,1... | collective-permute-start | bytes 786440 | tf_op jit(solution)/shard_map/ppermute | solution.py:261
  3.1 12.2 %collective-permute-start.1 = (f32[64,1024]{1,0:T(8,128)S(1)}, f32[64,1024]{1,0:T(8,128)S(1)}, u32[]{:S(2)}, u32[]{:S(2)}) collective-permute-start(f32[64,1024]{1,0:T(8,128)S(1)} %get-tuple-element.12), channel_id=1, source_target_pairs={{0,1},{1,0},{2,3},{3,2},{4,5},{5,4},{6,7},{7,6},{8,9},{9,8},{10,11... | collective-permute-start | bytes 786440 | tf_op jit(solution)/shard_map/ppermute | solution.py:260
  16.2 8.9 %collective-permute-start.2 = (f32[256,128]{1,0:T(8,128)S(1)}, f32[256,128]{1,0:T(8,128)S(1)}, u32[]{:S(2)}, u32[]{:S(2)}) collective-permute-start(f32[256,128]{1,0:T(8,128)S(1)} %get-tuple-element.15), channel_id=1, source_target_pairs={{0,32},{1,2},{2,1},{3,4},{4,3},{5,6},{6,5},{7,8},{8,7},{9,10},{10,... | collective-permute-start | bytes 393224 | tf_op jit(solution)/shard_map/ppermute | solution.py:272
  21.2 4.0 %collective-permute-start.3 = (f32[256,128]{1,0:T(8,128)S(1)}, f32[256,128]{1,0:T(8,128)S(1)}, u32[]{:S(2)}, u32[]{:S(2)}) collective-permute-start(f32[256,128]{1,0:T(8,128)S(1)} %get-tuple-element.16), channel_id=1, source_target_pairs={{0,1},{1,0},{2,3},{3,2},{4,5},{5,4},{6,7},{7,6},{8,9},{9,8},{10,11... | collective-permute-start | bytes 393224 | tf_op jit(solution)/shard_map/ppermute | solution.py:271
  21.2 4.0 %copy-start.1 = (bf16[4,512,512]{2,1,0:T(8,128)(2,1)S(1)}, bf16[4,512,512]{2,1,0:T(8,128)(2,1)}, u32[]{:S(2)}) copy-start(bf16[4,512,512]{2,1,0:T(8,128)(2,1)} %constant.5.clone.tab_ref) | copy-start | bytes 6291460

commit v3 on v2

--- a/solution.py
+++ b/solution.py
@@ -14,8 +14,9 @@
 HALO = 4
 TAPS = 9
 WIDE = COLS + 2 * HALO
-CHUNK = 12
+REST = COLS - HALO
 AXES = ("inline", "xline")
+AHEAD = (4, 5, 2, 0)
 
 
 def split_bf16(table):
@@ -72,14 +73,15 @@
 
 def filter_row(regs, ref, swapped_ref, in_base, inputs, acc_ref, out_base, outputs):
     spot = lambda base, n: pl.ds((base + n) * 8, 8)
-    acc = {t: acc_ref[spot(out_base, t), :] for t in outputs}
+    reach = lambda t: any(n <= t <= n + 2 * HALO for n in inputs)
+    acc = {t: acc_ref[spot(out_base, t), :] for t in outputs if reach(t)}
     for n in inputs:
         pairs = [(n - b + 2 * HALO, b) for b in range(TAPS) if n - b + 2 * HALO in acc]
         if pairs:
             x, xs = ref[spot(in_base, n), :], swapped_ref[spot(in_base, n), :]
             for t, b in pairs:
                 acc[t] = acc[t] + (regs[b] * x + regs[TAPS + b] * xs)
-    for t in outputs:
+    for t in acc:
         acc_ref[spot(out_base, t), :] = acc[t]
 
 
@@ -98,11 +100,35 @@
     return jnp.where(is_end, 0.0, 1.0).astype(jnp.float32)
 
 
-def edges_kernel(x_ref, far_ref, near_ref):
+def each_parity(body):
+    odd = parity_of("xline")
+    for parity in (0, 1):
+        pl.when(odd == parity)(lambda: body(parity))
+
+
+def side_columns(parity):
+    return range(COLS - HALO, COLS) if parity else range(HALO)
+
+
+def other_columns(parity):
+    return range(COLS - HALO) if parity else range(HALO, COLS)
+
+
+def edges_kernel(x_ref, far_side, near_side, far_rest, near_rest):
     odd_row = parity_of("inline")
-    for r in range(HALO):
-        far_ref[r * COLS : (r + 1) * COLS, :] = x_ref[HALO * odd_row + r]
-        near_ref[r * COLS : (r + 1) * COLS, :] = x_ref[HALO - HALO * odd_row + r]
+
+    def body(parity):
+        side, rest = side_columns(parity), other_columns(parity)
+        for first, side_ref, rest_ref in (
+            (HALO * odd_row, far_side, far_rest),
+            (HALO - HALO * odd_row, near_side, near_rest),
+        ):
+            for r in range(HALO):
+                row = first + r
+                side_ref[r * HALO : (r + 1) * HALO, :] = x_ref[row, side[0] : side[-1] + 1, :]
+                rest_ref[r * REST : (r + 1) * REST, :] = x_ref[row, rest[0] : rest[-1] + 1, :]
+
+    each_parity(body)
 
 
 def taps_kernel(f_ref, h_ref):
@@ -124,27 +150,6 @@
             h_ref[pl.ds(part * 8 + s + 4, count, stride=16), :] = value
 
 
-def filter_columns(regs, fr, fs, row, acc_ref, i):
-    for t0 in range(0, WIDE, CHUNK):
-        filter_row(regs, fr, fs, row * COLS, range(COLS), acc_ref, i * WIDE, range(t0, t0 + CHUNK))
-
-
-def own_kernel(x_ref, tab_ref, h_ref, acc_ref, fr, fs):
-    place(forward(x_ref[...].reshape(ROWS * COLS, NT), tab_ref), 0, ROWS * COLS, fr, fs, 0)
-    acc_ref[...] = jnp.zeros_like(acc_ref)
-
-    def tap_row(a, carry):
-        regs = load_taps(h_ref, a)
-
-        def out_row(i, carry):
-            filter_columns(regs, fr, fs, i + a - HALO, acc_ref, i)
-            return carry
-
-        return lax.fori_loop(jnp.maximum(0, HALO - a), jnp.minimum(ROWS, ROWS + HALO - a), out_row, carry)
-
-    lax.fori_loop(0, TAPS, tap_row, 0)
-
-
 def neighbour_rows(h_ref, below, body):
     for step in range(HALO):
         regs = load_taps(h_ref, step + (HALO + 1) * below)
@@ -157,61 +162,162 @@
         lax.fori_loop(first, HALO - step + (HALO + step) * below, out_row, 0)
 
 
-def near_kernel(acc_in, near_ref, tab_ref, h_ref, acc_ref, fr, fs):
+def own_rows(h_ref, body, first=0, last=TAPS):
+    def tap_row(a, carry):
+        regs = load_taps(h_ref, a)
+
+        def out_row(i, carry):
+            body(regs, i + a - HALO, i)
+            return carry
+
+        return lax.fori_loop(jnp.maximum(0, HALO - a), jnp.minimum(ROWS, ROWS + HALO - a), out_row, carry)
+
+    lax.fori_loop(first, last, tap_row, 0)
+
+
+def side_outputs(parity):
+    return range(COLS + HALO, WIDE) if parity else range(HALO)
+
+
+def spectra_kernel(x_ref, tab_ref, h_ref, fr, fs, side_ref):
+    place(forward(x_ref[...].reshape(ROWS * COLS, NT), tab_ref), 0, ROWS * COLS, fr, fs, 0)
+    side_ref[...] = jnp.zeros_like(side_ref)
+
+    def body(parity):
+        inputs, outputs = side_columns(parity), side_outputs(parity)
+
+        def out(regs, row, i):
+            filter_row(regs, fr, fs, row * COLS, inputs, side_ref, i * HALO - outputs[0], outputs)
+
+        own_rows(h_ref, out)
+
+    each_parity(body)
+
+
+def side_kernel(own_ref, near_ref, far_ref, tab_ref, h_ref, acc_ref, side_ref, nr, ns, fr, fs):
+    keep = keep_of("inline")
+    tiles = forward(jnp.concatenate([near_ref[...], far_ref[...]], axis=0), tab_ref)
+    count = HALO * HALO
+    place(tiles, 0, count, nr, ns, 0)
+    place([tile * keep for tile in tiles], count, count, fr, fs, 0)
+    side_ref[...] = own_ref[...]
+    far_below = parity_of("inline")
+
+    def body(parity):
+        inputs, outputs = side_columns(parity), side_outputs(parity)
+        for ref, swapped_ref, below in ((nr, ns, 1 - far_below), (fr, fs, far_below)):
+
+            def out(regs, row, i):
+                base = row * HALO - inputs[0]
+                filter_row(regs, ref, swapped_ref, base, inputs, side_ref, i * HALO - outputs[0], outputs)
+
+            neighbour_rows(h_ref, below, out)
+
+    each_parity(body)
+
+
+def halves(outputs):
+    middle = len(outputs) // 2
+    return outputs[:middle], outputs[middle:]
+
+
+def inner_outputs(parity):
+    return range(COLS + HALO) if parity else range(HALO, WIDE)
+
+
+def ahead():
+    place_in_run = lax.rem(lax.axis_index("xline"), 8)
+    count = jnp.where((place_in_run == 1) | (place_in_run == 3), AHEAD[1], AHEAD[3])
+    count = jnp.where(place_in_run == 0, AHEAD[0], count)
+    return jnp.where(place_in_run == 5, AHEAD[2], count)
+
+
+def filter_own(fr, fs, h_ref, acc_ref, first, last):
+    def body(parity):
+        def out(regs, row, i):
+            for outputs in halves(inner_outputs(parity)):
+                filter_row(regs, fr, fs, row * COLS, range(COLS), acc_ref, i * WIDE, outputs)
+
+        own_rows(h_ref, out, first, last)
+
+    each_parity(body)
+
+
+def early_kernel(fr, fs, h_ref, acc_ref):
+    acc_ref[...] = jnp.zeros_like(acc_ref)
+    filter_own(fr, fs, h_ref, acc_ref, 0, ahead())
+
+
+def late_kernel(acc_in, fr, fs, h_ref, acc_ref):
     acc_ref[...] = acc_in[...]
-    place(forward(near_ref[...], tab_ref), 0, HALO * COLS, fr, fs, 0)
-    neighbour_rows(
-        h_ref, 1 - parity_of("inline"), lambda regs, row, i: filter_columns(regs, fr, fs, row, acc_ref, i)
-    )
-
-
-def ends_kernel(acc_ref, far_ref, tab_ref, h_ref, side_ref, mate_ref, fr, fs):
+    filter_own(fr, fs, h_ref, acc_ref, ahead(), TAPS)
+
+
+def near_kernel(acc_in, rest_ref, nr, ns, tab_ref, h_ref, acc_ref, fr, fs):
+    acc_ref[...] = acc_in[...]
+    place(forward(rest_ref[...], tab_ref), 0, HALO * REST, fr, fs, 0)
+
+    def body(parity):
+        side, rest = side_columns(parity), other_columns(parity)
+
+        def out(regs, row, i):
+            for outputs in halves(inner_outputs(parity)):
+                filter_row(regs, nr, ns, row * HALO - side[0], side, acc_ref, i * WIDE, outputs)
+                filter_row(regs, fr, fs, row * REST - rest[0], rest, acc_ref, i * WIDE, outputs)
+
+        neighbour_rows(h_ref, 1 - parity_of("inline"), out)
+
+    each_parity(body)
+
+
+def mate_kernel(acc_ref, rest_ref, tab_ref, h_ref, mate_ref, fr, fs):
     keep = keep_of("inline")
-    tiles = [tile * keep for tile in forward(far_ref[...], tab_ref)]
-    place(tiles, 0, HALO * COLS, fr, fs, 0)
-
-    def body(parity):
-        left_ref, right_ref = (side_ref, mate_ref) if parity == 0 else (mate_ref, side_ref)
-        right = WIDE - HALO
+    place([tile * keep for tile in forward(rest_ref[...], tab_ref)], 0, HALO * REST, fr, fs, 0)
+
+    def body(parity):
+        outputs, rest = side_outputs(1 - parity), other_columns(parity)
+        inputs = side_columns(1 - parity)
         for i in range(ROWS):
-            target = pl.ds(i * HALO * 8, HALO * 8)
-            left_ref[target, :] = acc_ref[pl.ds(i * WIDE * 8, HALO * 8), :]
-            right_ref[target, :] = acc_ref[pl.ds((i * WIDE + right) * 8, HALO * 8), :]
-
-        def far_out(regs, row, i):
-            base = row * COLS
-            filter_row(regs, fr, fs, base, range(HALO), left_ref, i * HALO, range(HALO))
-            filter_row(
-                regs, fr, fs, base, range(COLS - HALO, COLS), right_ref, i * HALO - right, range(right, WIDE)
-            )
-
-        neighbour_rows(h_ref, parity_of("inline"), far_out)
-
+            source = pl.ds((i * WIDE + outputs[0]) * 8, HALO * 8)
+            mate_ref[pl.ds(i * HALO * 8, HALO * 8), :] = acc_ref[source, :]
+
+        def out(regs, row, i):
+            filter_row(regs, fr, fs, row * REST - rest[0], inputs, mate_ref, i * HALO - outputs[0], outputs)
+
+        neighbour_rows(h_ref, parity_of("inline"), out)
+
+    each_parity(body)
+
+
+def inner_kernel(acc_ref, rr, rs, sr, ss, h_ref, out_ref):
+    def body(parity):
+        side, rest = side_columns(parity), other_columns(parity)
+        for i in range(ROWS):
+            out_ref[pl.ds(i * COLS * 8, COLS * 8), :] = acc_ref[pl.ds((i * WIDE + HALO) * 8, COLS * 8), :]
+
+        def out(regs, row, i):
+            for outputs in halves(range(HALO, HALO + COLS)):
+                filter_row(regs, sr, ss, row * HALO - side[0], side, out_ref, i * COLS - HALO, outputs)
+                filter_row(regs, rr, rs, row * REST - rest[0], rest, out_ref, i * COLS - HALO, outputs)
+
+        neighbour_rows(h_ref, parity_of("inline"), out)
+
+    each_parity(body)
+
+
+def add_kernel(acc_ref, side_ref, out_ref):
+    odd, keep = parity_of("xline"), keep_of("xline")
+    out_ref[...] = acc_ref[...]
+    for i in range(ROWS):
+        target = pl.ds(pl.multiple_of((i * COLS + 12 * odd) * 8, 8), HALO * 8)
+        out_ref[target, :] = out_ref[target, :] + side_ref[pl.ds(i * HALO * 8, HALO * 8), :] * keep
+
+
+def inverse_kernel(acc_ref, mate_ref, tab_ref, out_ref, work):
     odd = parity_of("xline")
-    for parity in (0, 1):
-        pl.when(odd == parity)(lambda: body(parity))
-
-
-def inner_kernel(acc_ref, fr, fs, h_ref, out_ref):
-    for i in range(ROWS):
-        out_ref[pl.ds(i * COLS * 8, COLS * 8), :] = acc_ref[pl.ds((i * WIDE + HALO) * 8, COLS * 8), :]
-
-    def far_out(regs, row, i):
-        for t0 in (HALO, HALO + COLS // 2):
-            outputs = range(t0, t0 + COLS // 2)
-            filter_row(regs, fr, fs, row * COLS, range(COLS), out_ref, i * COLS - HALO, outputs)
-
-    neighbour_rows(h_ref, parity_of("inline"), far_out)
-
-
-def inverse_kernel(acc_ref, side_ref, mate_ref, tab_ref, out_ref, work):
-    odd = parity_of("xline")
-    keep = keep_of("xline")
     work[...] = acc_ref[...]
     for i in range(ROWS):
         source = pl.ds(i * HALO * 8, HALO * 8)
-        side = pl.ds(pl.multiple_of((i * COLS + 12 * odd) * 8, 8), HALO * 8)
-        work[side, :] = work[side, :] + side_ref[source, :] * keep
         mate = pl.ds(pl.multiple_of((i * COLS + 12 - 12 * odd) * 8, 8), HALO * 8)
         work[mate, :] = work[mate, :] + mate_ref[source, :]
     lane = lax.broadcasted_iota(jnp.int32, (ROWS * COLS, 128), 1)
@@ -226,10 +332,11 @@
     out_ref[:, :, HALF:] = (parts[0] - parts[1]).reshape(ROWS, COLS, HALF)
 
 
-def call(kernel, outs, scratch, args, weight=0):
+def call(kernel, outs, scratch, args, specs=None, weight=0):
     return pl.pallas_call(
         kernel,
         out_shape=[jax.ShapeDtypeStruct(shape, jnp.float32) for shape in outs],
+        in_specs=specs or [pl.BlockSpec()] * len(args),
         scratch_shapes=[pltpu.VMEM(shape, jnp.float32) for shape in scratch],
         compiler_params=pltpu.CompilerParams(vmem_limit_bytes=40 * 2**20),
         cost_estimate=pl.CostEstimate(flops=weight * 10**9, bytes_accessed=0, transcendentals=0) if weight else None,
@@ -255,23 +362,37 @@
     tab, inverse_tab = (jnp.asarray(table) for table in tables())
     taps = jnp.transpose(filters.reshape(2, HALF // 128, 128, TAPS * TAPS), (3, 1, 0, 2)).reshape(-1, 128)
 
-    rows = (HALO * COLS, NT)
-    to_far, to_near = call(edges_kernel, [rows, rows], [], (traces,), weight=2)
-    from_far = lax.ppermute(to_far, AXES, far)
-    from_near = lax.ppermute(to_near, "inline", near)
+    corner, rest = (HALO * HALO, NT), (HALO * REST, NT)
+    far_side, near_side, far_rest, near_rest = call(edges_kernel, [corner, corner, rest, rest], [], (traces,), weight=2)
+    far_side = lax.ppermute(far_side, AXES, far)
+    near_side = lax.ppermute(near_side, "inline", near)
+    far_rest = lax.ppermute(far_rest, AXES, far)
+    near_rest = lax.ppermute(near_rest, "inline", near)
 
     wide = (ROWS * WIDE * 8, 128)
     frame = (ROWS * COLS * 8, 128)
     spot = (ROWS * HALO * 8, 128)
-    rows_frame = (HALO * COLS * 8, 128)
-    (h,) = call(taps_kernel, [(2 * TAPS * TAPS * 8, 128)], [], (taps,), weight=1)
-    (acc,) = call(own_kernel, [wide], [frame, frame], (traces, tab, h), weight=10)
-    (acc,) = call(near_kernel, [wide], [rows_frame] * 2, (acc, from_near, tab, h), weight=2)
-    to_side, to_mate, fr, fs = call(ends_kernel, [spot, spot, rows_frame, rows_frame], [], (acc, from_far, tab, h))
+    side_frame = (HALO * HALO * 8, 128)
+    rest_frame = (HALO * REST * 8, 128)
+    (h,) = call(taps_kernel, [(2 * TAPS * TAPS * 8, 128)], [], (taps,))
+    fr, fs, to_side = call(spectra_kernel, [frame, frame, spot], [], (traces, tab, h))
+    (acc,) = call(early_kernel, [wide], [], (fr, fs, h))
+    vmem, anywhere = pl.BlockSpec(memory_space=pltpu.VMEM), pl.BlockSpec(memory_space=pl.ANY)
+    to_side, nr, ns, sr, ss = call(
+        side_kernel,
+        [spot] + [side_frame] * 4,
+        [],
+        (to_side, near_side, far_side, tab, h, acc),
+        specs=[vmem] * 5 + [anywhere],
+    )
+    from_side = lax.ppermute(to_side, AXES, side)
+    (acc,) = call(late_kernel, [wide], [], (acc, fr, fs, h), weight=20)
+    (acc,) = call(near_kernel, [wide], [rest_frame] * 2, (acc, near_rest, nr, ns, tab, h))
+    to_mate, rr, rs = call(mate_kernel, [spot, rest_frame, rest_frame], [], (acc, far_rest, tab, h))
     from_mate = lax.ppermute(to_mate, "xline", mate)
-    from_side = lax.ppermute(to_side, AXES, side)
-    (acc,) = call(inner_kernel, [frame], [], (acc, fr, fs, h), weight=2)
-    (out,) = call(inverse_kernel, [(ROWS, COLS, NT)], [frame], (acc, from_side, from_mate, inverse_tab))
+    (acc,) = call(inner_kernel, [frame], [], (acc, rr, rs, sr, ss, h), weight=1)
+    (acc,) = call(add_kernel, [frame], [], (acc, from_side), weight=5)
+    (out,) = call(inverse_kernel, [(ROWS, COLS, NT)], [frame], (acc, from_mate, inverse_tab))
     return out
 
 

time: 26.8 us -> 25.1 us (0.937)
  waiting for transfers between devices: 7.61 us -> 4.23 us
  Pallas kernels: 10.5 us -> 12 us
    ppermute x2 -> x4, waiting for transfers between devices: 4.4 us -> 0.01 us  [the longest x1 0.01 us: per_device(): near_side = lax.ppermute(near_side, 'inline', near)]
    ppermute x2 -> x4, starting transfers between devices: 2.38 us -> 4.93 us  [the longest x1 2.55 us: per_device(): far_rest = lax.ppermute(far_rest, AXES, far)]
    ppermute x1, starting transfers between devices: 4.96 us -> 2.47 us  [per_device(): from_side = lax.ppermute(to_side, AXES, side)]
    pallas_call x7 -> x11, Pallas kernels: 10.5 us -> 12 us  [call(): pl.pallas_call(kernel, out_shape=[jax.ShapeDtypeStruct(shape, jnp.float32...]
    ppermute x1, waiting for transfers between devices: 3.2 us -> 4.22 us  [per_device(): from_side = lax.ppermute(to_side, AXES, side)]
  transfers between devices with their start and end apart: 4 -> 6, of which waited for: 3 -> 1; matrix products, arithmetic and copies ran while one was open for 0% -> 0% of each run, Pallas kernels for 31% -> 42%
where the time goes in v3:
time: 25.1 us; the launch traced here: 24.9 us
  Pallas kernels  12 us (48%)
  starting transfers between devices  7.49 us (30%)
  waiting for transfers between devices  4.23 us (17%)
  local copies, waits for them, and re-layouts  1.06 us (4%)
    pallas_call x11, Pallas kernels, call(): pl.pallas_call(kernel, out_shape=[jax.ShapeDtypeStruct(shape, jnp.float32...  12 us
    ppermute x1, waiting for transfers between devices, per_device(): from_side = lax.ppermute(to_side, AXES, side)  4.22 us
    ppermute x1, starting transfers between devices, per_device(): far_rest = lax.ppermute(far_rest, AXES, far)  2.55 us
    ppermute x1, starting transfers between devices, per_device(): from_side = lax.ppermute(to_side, AXES, side)  2.47 us
    ppermute x1, starting transfers between devices, per_device(): near_side = lax.ppermute(near_side, 'inline', near)  2 us
    unnamed x10, local copies, waits for them, and re-layouts  1.06 us
  transfers between devices with their start and end apart: 6, of which 1 were waited for; matrix products, arithmetic and copies ran while one was open for 0% of the time, Pallas kernels for 42%

profile of v3, /device:TPU:30, one launch (start us, length us, event | category | flops | bytes accessed | tf_op | source)
XLA Modules:
  0.0 24.9 jit_solution(7018372456977313415)
XLA Ops:
  0.0 0.0 copy-start.2
  0.0 1.0 %copy-done.2 = f32[8,16,1024]{2,1,0:T(8,128)S(1)} copy-done((f32[8,16,1024]{2,1,0:T(8,128)S(1)}, f32[8,16,1024]{2,1,0:T(8,128)}, u32[]{:S(2)}) %copy-start.2) | copy-done | bytes 524312
  1.0 0.0 copy-start.4
  1.0 0.0 copy-start
  1.0 0.1 shard_map.50
  1.1 2.0 %collective-permute-start.1 = (f32[16,1024]{1,0:T(8,128)S(1)}, f32[16,1024]{1,0:T(8,128)S(1)}, u32[]{:S(2)}, u32[]{:S(2)}) collective-permute-start(f32[16,1024]{1,0:T(8,128)S(1)} %get-tuple-element.24), channel_id=1, source_target_pairs={{0,32},{32,0},{64,96},{96,64},{128,160},{160,128},{192,224},{224,1... | collective-permute-start | bytes 196616 | tf_op jit(solution)/shard_map/ppermute | solution.py:368
  3.1 0.4 %collective-permute-start.2 = (f32[16,1024]{1,0:T(8,128)S(1)}, f32[16,1024]{1,0:T(8,128)S(1)}, u32[]{:S(2)}, u32[]{:S(2)}) collective-permute-start(f32[16,1024]{1,0:T(8,128)S(1)} %get-tuple-element.25), channel_id=1, source_target_pairs={{0,1},{1,0},{2,3},{3,2},{4,5},{5,4},{6,7},{7,6},{8,9},{9,8},{10,11... | collective-permute-start | bytes 196616 | tf_op jit(solution)/shard_map/ppermute | solution.py:367
  3.5 0.0 collective-permute-start
  3.5 2.6 %collective-permute-start.3 = (f32[48,1024]{1,0:T(8,128)S(1)}, f32[48,1024]{1,0:T(8,128)S(1)}, u32[]{:S(2)}, u32[]{:S(2)}) collective-permute-start(f32[48,1024]{1,0:T(8,128)S(1)} %get-tuple-element.28), channel_id=1, source_target_pairs={{0,1},{1,0},{2,3},{3,2},{4,5},{5,4},{6,7},{7,6},{8,9},{9,8},{10,11... | collective-permute-start | bytes 589832 | tf_op jit(solution)/shard_map/ppermute | solution.py:369
  6.1 0.0 copy-done.4
  6.1 0.8 %shard_map.46.h_ref = f32[1296,128]{1,0:T(8,128)S(1)} custom-call(f32[648,128]{1,0:T(8,128)S(1)} %bitcast.5), custom_call_target="tpu_custom_call" | custom-call | tf_op jit(solution)/shard_map/pallas_call | solution.py:336
  6.9 0.0 copy-done
  6.9 0.0 copy-done.3
  6.9 1.5 %shard_map.47 = (f32[1024,128]{1,0:T(8,128)S(1)}, f32[1024,128]{1,0:T(8,128)S(1)}, f32[256,128]{1,0:T(8,128)S(1)}) custom-call(f32[8,16,1024]{2,1,0:T(8,128)S(1)} %copy-done.3, bf16[4,512,512]{2,1,0:T(8,128)(2,1)S(1)} %copy-done, f32[1296,128]{1,0:T(8,128)S(1)} %shard_map.46.h_ref), custom_call_target="tpu_custom_call" | custom-call | tf_op jit(solution)/shard_map/pallas_call | solution.py:336
  8.4 1.8 %shard_map.48.acc_in.acc_ref = f32[1536,128]{1,0:T(8,128)S(1)} custom-call(f32[1024,128]{1,0:T(8,128)S(1)} %get-tuple-element.20.fr, f32[1024,128]{1,0:T(8,128)S(1)} %get-tuple-element.21.fs, f32[1296,128]{1,0:T(8,128)S(1)} %shard_map.46.h_ref), custom_call_target="tpu_custom_call" | custom-call | tf_op jit(solution)/shard_map/pallas_call | solution.py:336
  10.1 0.0 collective-permute-done.1.near_ref
  10.1 0.0 collective-permute-done.2.far_ref
  10.1 0.9 %shard_map.51 = (f32[256,128]{1,0:T(8,128)S(1)}, f32[128,128]{1,0:T(8,128)S(1)}, f32[128,128]{1,0:T(8,128)S(1)}, f32[128,128]{1,0:T(8,128)S(1)}, f32[128,128]{1,0:T(8,128)S(1)}) custom-call(f32[256,128]{1,0:T(8,128)S(1)} %get-tuple-element.23.own_ref, f32[16,1024]{1,0:T(8,128)S(1)} %collective-permute-done.1.near_ref, ...), custom_call_target="tpu_custom_call" | custom-call | tf_op jit(solution)/shard_map/pallas_call | solution.py:336
  11.1 2.5 %collective-permute-start.4 = (f32[256,128]{1,0:T(8,128)S(1)}, f32[256,128]{1,0:T(8,128)S(1)}, u32[]{:S(2)}, u32[]{:S(2)}) collective-permute-start(f32[256,128]{1,0:T(8,128)S(1)} %get-tuple-element.33), channel_id=1, source_target_pairs={{0,32},{1,2},{2,1},{3,4},{4,3},{5,6},{6,5},{7,8},{8,7},{9,10},{10,... | collective-permute-start | bytes 393224 | tf_op jit(solution)/shard_map/ppermute | solution.py:388
  13.6 2.4 %shard_map.49.acc_in = f32[1536,128]{1,0:T(8,128)S(1)} custom-call(f32[1536,128]{1,0:T(8,128)S(1)} %shard_map.48.acc_in.acc_ref, f32[1024,128]{1,0:T(8,128)S(1)} %get-tuple-element.20.fr, f32[1024,128]{1,0:T(8,128)S(1)} %get-tuple-element.21.fs, f32[1296,128]{1,0:T(8,128)S(1)} %shard_map.46.h_ref), custom_call_target="tpu_custom_call" | custom-call | flops 20000000000 | tf_op jit(solution)/shard_map/pallas_call | solution.py:336
  15.9 0.0 collective-permute-done.rest_ref
  16.0 1.5 %shard_map.52.acc_ref = f32[1536,128]{1,0:T(8,128)S(1)} custom-call(f32[1536,128]{1,0:T(8,128)S(1)} %shard_map.49.acc_in, f32[48,1024]{1,0:T(8,128)S(1)} %collective-permute-done.rest_ref, f32[128,128]{1,0:T(8,128)S(1)} %get-tuple-element.26.nr, f32[128,128]{1,0:T(8,128)S(1)} %get-tuple-element.27.ns, bf16[4,512,512]{2,1,0:T(8,128)(2,1)S(1)} %copy-done, ...), custom_call_target="tpu_custom_call" | custom-call | tf_op jit(solution)/shard_map/pallas_call | solution.py:336
  17.5 0.0 collective-permute-done.3.rest_ref
  17.5 0.8 %shard_map.53 = (f32[256,128]{1,0:T(8,128)S(1)}, f32[384,128]{1,0:T(8,128)S(1)}, f32[384,128]{1,0:T(8,128)S(1)}) custom-call(f32[1536,128]{1,0:T(8,128)S(1)} %shard_map.52.acc_ref, f32[48,1024]{1,0:T(8,128)S(1)} %collective-permute-done.3.rest_ref, bf16[4,512,512]{2,1,0:T(8,128)(2,1)S(1)} %copy-done, f32[1296,128]{1,0:T(8,128)S(1)} %shard_map.46.h_ref), custom_call_target="tpu_custom_call" | custom-call | tf_op jit(solution)/shard_map/pallas_call | solution.py:336
  18.3 0.1 collective-permute-start.5
  18.4 0.8 %shard_map.54.acc_ref = f32[1024,128]{1,0:T(8,128)S(1)} custom-call(f32[1536,128]{1,0:T(8,128)S(1)} %shard_map.52.acc_ref, f32[384,128]{1,0:T(8,128)S(1)} %get-tuple-element.29.rr, f32[384,128]{1,0:T(8,128)S(1)} %get-tuple-element.30.rs, f32[128,128]{1,0:T(8,128)S(1)} %get-tuple-element.31.sr, f32[128,128]{1,0:T(8,128)S(1)} %get-tuple-element.32.ss, ...), custom_call_target="tpu_custom_call" | custom-call | flops 1000000000 | tf_op jit(solution)/shard_map/pallas_call | solution.py:336
  19.2 0.0 copy-start.1
  19.2 4.2 %collective-permute-done.4.side_ref = f32[256,128]{1,0:T(8,128)S(1)} collective-permute-done((f32[256,128]{1,0:T(8,128)S(1)}, f32[256,128]{1,0:T(8,128)S(1)}, u32[]{:S(2)}, u32[]{:S(2)}) %collective-permute-start.4) | collective-permute-done | bytes 131104 | tf_op jit(solution)/shard_map/ppermute | solution.py:388
  23.4 0.1 shard_map.55.acc_ref
  23.5 0.0 collective-permute-done.5.mate_ref
  23.5 0.0 copy-done.1
  23.5 1.4 %shard_map.56 = f32[8,16,1024]{2,1,0:T(8,128)} custom-call(f32[1024,128]{1,0:T(8,128)S(1)} %shard_map.55.acc_ref, f32[256,128]{1,0:T(8,128)S(1)} %collective-permute-done.5.mate_ref, bf16[4,512,512]{2,1,0:T(8,128)(2,1)S(1)} %copy-done.1), custom_call_target="tpu_custom_call" | custom-call | tf_op jit(solution)/shard_map/pallas_call | solution.py:336
  (1 shorter events, 0.0 us)
Async XLA Ops:
  0.0 1.0 %copy-start.2 = (f32[8,16,1024]{2,1,0:T(8,128)S(1)}, f32[8,16,1024]{2,1,0:T(8,128)}, u32[]{:S(2)}) copy-start(f32[8,16,1024]{2,1,0:T(8,128)} %x_ref.3) | copy-start | bytes 1572868
  1.0 5.0 %copy-start.4 = (f32[2,512,81]{1,0,2:T(2,128)S(1)}, f32[2,512,81]{1,0,2:T(2,128)}, u32[]{:S(2)}) copy-start(f32[2,512,81]{1,0,2:T(2,128)} %param.5) | copy-start | bytes 995332
  1.0 5.8 %copy-start = (bf16[4,512,512]{2,1,0:T(8,128)(2,1)S(1)}, bf16[4,512,512]{2,1,0:T(8,128)(2,1)}, u32[]{:S(2)}) copy-start(bf16[4,512,512]{2,1,0:T(8,128)(2,1)} %constant.4.clone.tab_ref) | copy-start | bytes 6291460
  1.0 5.8 %copy-start.3 = (f32[8,16,1024]{2,1,0:T(8,128)S(1)}, f32[8,16,1024]{2,1,0:T(8,128)}, u32[]{:S(2)}) copy-start(f32[8,16,1024]{2,1,0:T(8,128)} %x_ref.3) | copy-start | bytes 1572868
  1.1 9.0 %collective-permute-start.1 = (f32[16,1024]{1,0:T(8,128)S(1)}, f32[16,1024]{1,0:T(8,128)S(1)}, u32[]{:S(2)}, u32[]{:S(2)}) collective-permute-start(f32[16,1024]{1,0:T(8,128)S(1)} %get-tuple-element.24), channel_id=1, source_target_pairs={{0,32},{32,0},{64,96},{96,64},{128,160},{160,128},{192,224},{224,1... | collective-permute-start | bytes 196616 | tf_op jit(solution)/shard_map/ppermute | solution.py:368
  3.1 7.0 %collective-permute-start.2 = (f32[16,1024]{1,0:T(8,128)S(1)}, f32[16,1024]{1,0:T(8,128)S(1)}, u32[]{:S(2)}, u32[]{:S(2)}) collective-permute-start(f32[16,1024]{1,0:T(8,128)S(1)} %get-tuple-element.25), channel_id=1, source_target_pairs={{0,1},{1,0},{2,3},{3,2},{4,5},{5,4},{6,7},{7,6},{8,9},{9,8},{10,11... | collective-permute-start | bytes 196616 | tf_op jit(solution)/shard_map/ppermute | solution.py:367
  3.5 12.4 %collective-permute-start = (f32[48,1024]{1,0:T(8,128)S(1)}, f32[48,1024]{1,0:T(8,128)S(1)}, u32[]{:S(2)}, u32[]{:S(2)}) collective-permute-start(f32[48,1024]{1,0:T(8,128)S(1)} %get-tuple-element.22), channel_id=1, source_target_pairs={{0,32},{32,0},{64,96},{96,64},{128,160},{160,128},{192,224},{224,1... | collective-permute-start | bytes 589832 | tf_op jit(solution)/shard_map/ppermute | solution.py:370
  3.5 14.0 %collective-permute-start.3 = (f32[48,1024]{1,0:T(8,128)S(1)}, f32[48,1024]{1,0:T(8,128)S(1)}, u32[]{:S(2)}, u32[]{:S(2)}) collective-permute-start(f32[48,1024]{1,0:T(8,128)S(1)} %get-tuple-element.28), channel_id=1, source_target_pairs={{0,1},{1,0},{2,3},{3,2},{4,5},{5,4},{6,7},{7,6},{8,9},{9,8},{10,11... | collective-permute-start | bytes 589832 | tf_op jit(solution)/shard_map/ppermute | solution.py:369
  11.1 12.3 %collective-permute-start.4 = (f32[256,128]{1,0:T(8,128)S(1)}, f32[256,128]{1,0:T(8,128)S(1)}, u32[]{:S(2)}, u32[]{:S(2)}) collective-permute-start(f32[256,128]{1,0:T(8,128)S(1)} %get-tuple-element.33), channel_id=1, source_target_pairs={{0,32},{1,2},{2,1},{3,4},{4,3},{5,6},{6,5},{7,8},{8,7},{9,10},{10,... | collective-permute-start | bytes 393224 | tf_op jit(solution)/shard_map/ppermute | solution.py:388
  18.3 5.2 %collective-permute-start.5 = (f32[256,128]{1,0:T(8,128)S(1)}, f32[256,128]{1,0:T(8,128)S(1)}, u32[]{:S(2)}, u32[]{:S(2)}) collective-permute-start(f32[256,128]{1,0:T(8,128)S(1)} %get-tuple-element.34), channel_id=1, source_target_pairs={{0,1},{1,0},{2,3},{3,2},{4,5},{5,4},{6,7},{7,6},{8,9},{9,8},{10,11... | collective-permute-start | bytes 393224 | tf_op jit(solution)/shard_map/ppermute | solution.py:392
  19.2 4.3 %copy-start.1 = (bf16[4,512,512]{2,1,0:T(8,128)(2,1)S(1)}, bf16[4,512,512]{2,1,0:T(8,128)(2,1)}, u32[]{:S(2)}) copy-start(bf16[4,512,512]{2,1,0:T(8,128)(2,1)} %constant.5.clone.tab_ref) | copy-start | bytes 6291460

commit v4 on v3

--- a/solution.py
+++ b/solution.py
@@ -34,7 +34,7 @@
         table = np.concatenate([np.cos(phase), -np.sin(phase)], axis=1)
         out.extend(split_bf16(table))
         transposed.extend(split_bf16(table.T))
-    return np.stack(out), np.stack(transposed)
+    return np.stack(out + transposed)
 
 
 SUBLANE = ((0, 1, 4, 5), (2, 3, 6, 7))
@@ -114,21 +114,19 @@
     return range(COLS - HALO) if parity else range(HALO, COLS)
 
 
-def edges_kernel(x_ref, far_side, near_side, far_rest, near_rest):
+def edges_kernel(x_ref, far_side, far_rest, near_rows):
     odd_row = parity_of("inline")
 
     def body(parity):
         side, rest = side_columns(parity), other_columns(parity)
-        for first, side_ref, rest_ref in (
-            (HALO * odd_row, far_side, far_rest),
-            (HALO - HALO * odd_row, near_side, near_rest),
-        ):
-            for r in range(HALO):
-                row = first + r
-                side_ref[r * HALO : (r + 1) * HALO, :] = x_ref[row, side[0] : side[-1] + 1, :]
-                rest_ref[r * REST : (r + 1) * REST, :] = x_ref[row, rest[0] : rest[-1] + 1, :]
-
-    each_parity(body)
+        for r in range(HALO):
+            row = HALO * odd_row + r
+            far_side[r * HALO : (r + 1) * HALO, :] = x_ref[row, side[0] : side[-1] + 1, :]
+            far_rest[r * REST : (r + 1) * REST, :] = x_ref[row, rest[0] : rest[-1] + 1, :]
+
+    each_parity(body)
+    for r in range(HALO):
+        near_rows[r * COLS : (r + 1) * COLS, :] = x_ref[HALO - HALO * odd_row + r]
 
 
 def taps_kernel(f_ref, h_ref):
@@ -197,21 +195,23 @@
 def side_kernel(own_ref, near_ref, far_ref, tab_ref, h_ref, acc_ref, side_ref, nr, ns, fr, fs):
     keep = keep_of("inline")
     tiles = forward(jnp.concatenate([near_ref[...], far_ref[...]], axis=0), tab_ref)
-    count = HALO * HALO
-    place(tiles, 0, count, nr, ns, 0)
-    place([tile * keep for tile in tiles], count, count, fr, fs, 0)
+    place(tiles, 0, HALO * COLS, nr, ns, 0)
+    place([tile * keep for tile in tiles], HALO * COLS, HALO * HALO, fr, fs, 0)
     side_ref[...] = own_ref[...]
     far_below = parity_of("inline")
 
     def body(parity):
         inputs, outputs = side_columns(parity), side_outputs(parity)
-        for ref, swapped_ref, below in ((nr, ns, 1 - far_below), (fr, fs, far_below)):
-
-            def out(regs, row, i):
-                base = row * HALO - inputs[0]
-                filter_row(regs, ref, swapped_ref, base, inputs, side_ref, i * HALO - outputs[0], outputs)
-
-            neighbour_rows(h_ref, below, out)
+
+        def near_out(regs, row, i):
+            filter_row(regs, nr, ns, row * COLS, inputs, side_ref, i * HALO - outputs[0], outputs)
+
+        def far_out(regs, row, i):
+            base = row * HALO - inputs[0]
+            filter_row(regs, fr, fs, base, inputs, side_ref, i * HALO - outputs[0], outputs)
+
+        neighbour_rows(h_ref, 1 - far_below, near_out)
+        neighbour_rows(h_ref, far_below, far_out)
 
     each_parity(body)
 
@@ -253,17 +253,13 @@
     filter_own(fr, fs, h_ref, acc_ref, ahead(), TAPS)
 
 
-def near_kernel(acc_in, rest_ref, nr, ns, tab_ref, h_ref, acc_ref, fr, fs):
+def near_kernel(acc_in, nr, ns, h_ref, acc_ref):
     acc_ref[...] = acc_in[...]
-    place(forward(rest_ref[...], tab_ref), 0, HALO * REST, fr, fs, 0)
-
-    def body(parity):
-        side, rest = side_columns(parity), other_columns(parity)
-
+
+    def body(parity):
         def out(regs, row, i):
             for outputs in halves(inner_outputs(parity)):
-                filter_row(regs, nr, ns, row * HALO - side[0], side, acc_ref, i * WIDE, outputs)
-                filter_row(regs, fr, fs, row * REST - rest[0], rest, acc_ref, i * WIDE, outputs)
+                filter_row(regs, nr, ns, row * COLS, range(COLS), acc_ref, i * WIDE, outputs)
 
         neighbour_rows(h_ref, 1 - parity_of("inline"), out)
 
@@ -327,7 +323,7 @@
         if parity == 0:
             tiles[0] = jnp.where(lane == 0, 0.5 * tiles[0], tiles[0])
         spectrum = jnp.concatenate(tiles, axis=1)
-        parts.append(dot3(spectrum, tab_ref[2 * parity], tab_ref[2 * parity + 1]) * (2.0 / NT))
+        parts.append(dot3(spectrum, tab_ref[4 + 2 * parity], tab_ref[5 + 2 * parity]) * (2.0 / NT))
     out_ref[:, :, :HALF] = (parts[0] + parts[1]).reshape(ROWS, COLS, HALF)
     out_ref[:, :, HALF:] = (parts[0] - parts[1]).reshape(ROWS, COLS, HALF)
 
@@ -359,40 +355,40 @@
 
 def per_device(traces, filters):
     side, far, near, mate = permutations(lax.axis_size("inline"), lax.axis_size("xline"))
-    tab, inverse_tab = (jnp.asarray(table) for table in tables())
+    tab = jnp.asarray(tables())
     taps = jnp.transpose(filters.reshape(2, HALF // 128, 128, TAPS * TAPS), (3, 1, 0, 2)).reshape(-1, 128)
 
-    corner, rest = (HALO * HALO, NT), (HALO * REST, NT)
-    far_side, near_side, far_rest, near_rest = call(edges_kernel, [corner, corner, rest, rest], [], (traces,), weight=2)
+    corner, rest, rows = ((HALO * columns, NT) for columns in (HALO, REST, COLS))
+    far_side, far_rest, near_rows = call(edges_kernel, [corner, rest, rows], [], (traces,), weight=2)
     far_side = lax.ppermute(far_side, AXES, far)
-    near_side = lax.ppermute(near_side, "inline", near)
+    near_rows = lax.ppermute(near_rows, "inline", near)
     far_rest = lax.ppermute(far_rest, AXES, far)
-    near_rest = lax.ppermute(near_rest, "inline", near)
 
     wide = (ROWS * WIDE * 8, 128)
     frame = (ROWS * COLS * 8, 128)
     spot = (ROWS * HALO * 8, 128)
     side_frame = (HALO * HALO * 8, 128)
     rest_frame = (HALO * REST * 8, 128)
+    rows_frame = (HALO * COLS * 8, 128)
     (h,) = call(taps_kernel, [(2 * TAPS * TAPS * 8, 128)], [], (taps,))
     fr, fs, to_side = call(spectra_kernel, [frame, frame, spot], [], (traces, tab, h))
     (acc,) = call(early_kernel, [wide], [], (fr, fs, h))
     vmem, anywhere = pl.BlockSpec(memory_space=pltpu.VMEM), pl.BlockSpec(memory_space=pl.ANY)
     to_side, nr, ns, sr, ss = call(
         side_kernel,
-        [spot] + [side_frame] * 4,
+        [spot] + [rows_frame] * 2 + [side_frame] * 2,
         [],
-        (to_side, near_side, far_side, tab, h, acc),
+        (to_side, near_rows, far_side, tab, h, acc),
         specs=[vmem] * 5 + [anywhere],
     )
     from_side = lax.ppermute(to_side, AXES, side)
     (acc,) = call(late_kernel, [wide], [], (acc, fr, fs, h), weight=20)
-    (acc,) = call(near_kernel, [wide], [rest_frame] * 2, (acc, near_rest, nr, ns, tab, h))
+    (acc,) = call(near_kernel, [wide], [], (acc, nr, ns, h))
     to_mate, rr, rs = call(mate_kernel, [spot, rest_frame, rest_frame], [], (acc, far_rest, tab, h))
     from_mate = lax.ppermute(to_mate, "xline", mate)
     (acc,) = call(inner_kernel, [frame], [], (acc, rr, rs, sr, ss, h), weight=1)
-    (acc,) = call(add_kernel, [frame], [], (acc, from_side), weight=5)
-    (out,) = call(inverse_kernel, [(ROWS, COLS, NT)], [frame], (acc, from_mate, inverse_tab))
+    (acc,) = call(add_kernel, [frame], [], (acc, from_side), weight=1)
+    (out,) = call(inverse_kernel, [(ROWS, COLS, NT)], [frame], (acc, from_mate, tab))
     return out
 
 

time: 25.1 us -> 24.9 us (level)
  starting transfers between devices: 7.49 us -> 8.69 us
  waiting for transfers between devices: 4.23 us -> 3.43 us
  Pallas kernels: 12 us -> 11.3 us
    ppermute x1, waiting for transfers between devices: 4.22 us -> 1.49 us  [per_device(): from_side = lax.ppermute(to_side, AXES, side)]
    ppermute x1, waiting for transfers between devices: 0.01 us -> 1.93 us  [per_device(): far_side = lax.ppermute(far_side, AXES, far)]
    ppermute x1, starting transfers between devices: 2.47 us -> 3.67 us  [per_device(): from_side = lax.ppermute(to_side, AXES, side)]
    pallas_call x11, Pallas kernels: 12 us -> 11.3 us  [call(): pl.pallas_call(kernel, out_shape=[jax.ShapeDtypeStruct(shape, jnp.float32...]
    unnamed x10 -> x8, local copies, waits for them, and re-layouts: 1.06 us -> 1.2 us
    ppermute x2 -> x1, starting transfers between devices: 2.01 us -> 2 us  [per_device(): near_rows = lax.ppermute(near_rows, 'inline', near)]
  transfers between devices with their start and end apart: 6 -> 5, of which waited for: 1 -> 2; matrix products, arithmetic and copies ran while one was open for 0% -> 0% of each run, Pallas kernels for 42% -> 40%
where the time goes in v4:
time: 24.9 us; the launch traced here: 24.8 us
  Pallas kernels  11.3 us (45%)
  starting transfers between devices  8.69 us (35%)
  waiting for transfers between devices  3.43 us (14%)
  local copies, waits for them, and re-layouts  1.2 us (5%)
    pallas_call x11, Pallas kernels, call(): pl.pallas_call(kernel, out_shape=[jax.ShapeDtypeStruct(shape, jnp.float32...  11.3 us
    ppermute x1, starting transfers between devices, per_device(): from_side = lax.ppermute(to_side, AXES, side)  3.67 us
    ppermute x1, starting transfers between devices, per_device(): far_rest = lax.ppermute(far_rest, AXES, far)  2.55 us
    ppermute x1, starting transfers between devices, per_device(): near_rows = lax.ppermute(near_rows, 'inline', near)  2 us
    ppermute x1, waiting for transfers between devices, per_device(): far_side = lax.ppermute(far_side, AXES, far)  1.93 us
    ppermute x1, waiting for transfers between devices, per_device(): from_side = lax.ppermute(to_side, AXES, side)  1.49 us
    unnamed x8, local copies, waits for them, and re-layouts  1.2 us
  transfers between devices with their start and end apart: 5, of which 2 were waited for; matrix products, arithmetic and copies ran while one was open for 0% of the time, Pallas kernels for 40%

profile of v4, /device:TPU:30, one launch (start us, length us, event | category | flops | bytes accessed | tf_op | source)
XLA Modules:
  0.0 24.8 jit_solution(260510464228885273)
XLA Ops:
  0.0 0.0 copy-start
  0.0 0.0 copy-start.1
  0.0 1.2 %copy-done.1 = f32[8,16,1024]{2,1,0:T(8,128)S(1)} copy-done((f32[8,16,1024]{2,1,0:T(8,128)S(1)}, f32[8,16,1024]{2,1,0:T(8,128)}, u32[]{:S(2)}) %copy-start.1) | copy-done | bytes 524312
  1.2 0.0 copy-start.3
  1.2 0.0 copy-start.2
  1.2 0.1 shard_map.41
  1.3 2.0 %collective-permute-start = (f32[64,1024]{1,0:T(8,128)S(1)}, f32[64,1024]{1,0:T(8,128)S(1)}, u32[]{:S(2)}, u32[]{:S(2)}) collective-permute-start(f32[64,1024]{1,0:T(8,128)S(1)} %get-tuple-element.22), channel_id=1, source_target_pairs={{0,32},{32,0},{64,96},{96,64},{128,160},{160,128},{192,224},{224,1... | collective-permute-start | bytes 786440 | tf_op jit(solution)/shard_map/ppermute | solution.py:364
  3.3 0.4 %collective-permute-start.1 = (f32[16,1024]{1,0:T(8,128)S(1)}, f32[16,1024]{1,0:T(8,128)S(1)}, u32[]{:S(2)}, u32[]{:S(2)}) collective-permute-start(f32[16,1024]{1,0:T(8,128)S(1)} %get-tuple-element.23), channel_id=1, source_target_pairs={{0,1},{1,0},{2,3},{3,2},{4,5},{5,4},{6,7},{7,6},{8,9},{9,8},{10,11... | collective-permute-start | bytes 196616 | tf_op jit(solution)/shard_map/ppermute | solution.py:363
  3.6 2.6 %collective-permute-start.2 = (f32[48,1024]{1,0:T(8,128)S(1)}, f32[48,1024]{1,0:T(8,128)S(1)}, u32[]{:S(2)}, u32[]{:S(2)}) collective-permute-start(f32[48,1024]{1,0:T(8,128)S(1)} %get-tuple-element.26), channel_id=1, source_target_pairs={{0,1},{1,0},{2,3},{3,2},{4,5},{5,4},{6,7},{7,6},{8,9},{9,8},{10,11... | collective-permute-start | bytes 589832 | tf_op jit(solution)/shard_map/ppermute | solution.py:365
  6.2 0.0 copy-done.3
  6.2 0.8 %shard_map.37.h_ref = f32[1296,128]{1,0:T(8,128)S(1)} custom-call(f32[648,128]{1,0:T(8,128)S(1)} %bitcast.5), custom_call_target="tpu_custom_call" | custom-call | tf_op jit(solution)/shard_map/pallas_call | solution.py:332
  7.0 0.0 copy-done
  7.0 0.0 copy-done.2
  7.0 1.5 %shard_map.38 = (f32[1024,128]{1,0:T(8,128)S(1)}, f32[1024,128]{1,0:T(8,128)S(1)}, f32[256,128]{1,0:T(8,128)S(1)}) custom-call(f32[8,16,1024]{2,1,0:T(8,128)S(1)} %copy-done.2, bf16[8,512,512]{2,1,0:T(8,128)(2,1)S(1)} %copy-done, f32[1296,128]{1,0:T(8,128)S(1)} %shard_map.37.h_ref), custom_call_target="tpu_custom_call" | custom-call | tf_op jit(solution)/shard_map/pallas_call | solution.py:332
  8.5 1.8 %shard_map.39.acc_in.acc_ref = f32[1536,128]{1,0:T(8,128)S(1)} custom-call(f32[1024,128]{1,0:T(8,128)S(1)} %get-tuple-element.19.fr, f32[1024,128]{1,0:T(8,128)S(1)} %get-tuple-element.20.fs, f32[1296,128]{1,0:T(8,128)S(1)} %shard_map.37.h_ref), custom_call_target="tpu_custom_call" | custom-call | tf_op jit(solution)/shard_map/pallas_call | solution.py:332
  10.3 1.9 %collective-permute-done.1.far_ref = f32[16,1024]{1,0:T(8,128)S(1)} collective-permute-done((f32[16,1024]{1,0:T(8,128)S(1)}, f32[16,1024]{1,0:T(8,128)S(1)}, u32[]{:S(2)}, u32[]{:S(2)}) %collective-permute-start.1) | collective-permute-done | bytes 65568 | tf_op jit(solution)/shard_map/ppermute | solution.py:363
  12.2 0.0 collective-permute-done.near_ref
  12.2 1.0 %shard_map.42 = (f32[256,128]{1,0:T(8,128)S(1)}, f32[512,128]{1,0:T(8,128)S(1)}, f32[512,128]{1,0:T(8,128)S(1)}, f32[128,128]{1,0:T(8,128)S(1)}, f32[128,128]{1,0:T(8,128)S(1)}) custom-call(f32[256,128]{1,0:T(8,128)S(1)} %get-tuple-element.21.own_ref, f32[64,1024]{1,0:T(8,128)S(1)} %collective-permute-done.near_ref, ...), custom_call_target="tpu_custom_call" | custom-call | tf_op jit(solution)/shard_map/pallas_call | solution.py:332
  13.2 3.7 %collective-permute-start.3 = (f32[256,128]{1,0:T(8,128)S(1)}, f32[256,128]{1,0:T(8,128)S(1)}, u32[]{:S(2)}, u32[]{:S(2)}) collective-permute-start(f32[256,128]{1,0:T(8,128)S(1)} %get-tuple-element.31), channel_id=1, source_target_pairs={{0,32},{1,2},{2,1},{3,4},{4,3},{5,6},{6,5},{7,8},{8,7},{9,10},{10,... | collective-permute-start | bytes 393224 | tf_op jit(solution)/shard_map/ppermute | solution.py:384
  16.9 2.4 %shard_map.40.acc_in = f32[1536,128]{1,0:T(8,128)S(1)} custom-call(f32[1536,128]{1,0:T(8,128)S(1)} %shard_map.39.acc_in.acc_ref, f32[1024,128]{1,0:T(8,128)S(1)} %get-tuple-element.19.fr, f32[1024,128]{1,0:T(8,128)S(1)} %get-tuple-element.20.fs, f32[1296,128]{1,0:T(8,128)S(1)} %shard_map.37.h_ref), custom_call_target="tpu_custom_call" | custom-call | flops 20000000000 | tf_op jit(solution)/shard_map/pallas_call | solution.py:332
  19.2 0.8 %shard_map.43.acc_ref = f32[1536,128]{1,0:T(8,128)S(1)} custom-call(f32[1536,128]{1,0:T(8,128)S(1)} %shard_map.40.acc_in, f32[512,128]{1,0:T(8,128)S(1)} %get-tuple-element.24.nr, f32[512,128]{1,0:T(8,128)S(1)} %get-tuple-element.25.ns, f32[1296,128]{1,0:T(8,128)S(1)} %shard_map.37.h_ref), custom_call_target="tpu_custom_call" | custom-call | tf_op jit(solution)/shard_map/pallas_call | solution.py:332
  20.1 0.0 collective-permute-done.2.rest_ref
  20.1 0.8 %shard_map.44 = (f32[256,128]{1,0:T(8,128)S(1)}, f32[384,128]{1,0:T(8,128)S(1)}, f32[384,128]{1,0:T(8,128)S(1)}) custom-call(f32[1536,128]{1,0:T(8,128)S(1)} %shard_map.43.acc_ref, f32[48,1024]{1,0:T(8,128)S(1)} %collective-permute-done.2.rest_ref, bf16[8,512,512]{2,1,0:T(8,128)(2,1)S(1)} %copy-done, f32[1296,128]{1,0:T(8,128)S(1)} %shard_map.37.h_ref), custom_call_target="tpu_custom_call" | custom-call | tf_op jit(solution)/shard_map/pallas_call | solution.py:332
  20.9 0.1 collective-permute-start.4
  21.0 0.8 %shard_map.45.acc_ref = f32[1024,128]{1,0:T(8,128)S(1)} custom-call(f32[1536,128]{1,0:T(8,128)S(1)} %shard_map.43.acc_ref, f32[384,128]{1,0:T(8,128)S(1)} %get-tuple-element.27.rr, f32[384,128]{1,0:T(8,128)S(1)} %get-tuple-element.28.rs, f32[128,128]{1,0:T(8,128)S(1)} %get-tuple-element.29.sr, f32[128,128]{1,0:T(8,128)S(1)} %get-tuple-element.30.ss, ...), custom_call_target="tpu_custom_call" | custom-call | flops 1000000000 | tf_op jit(solution)/shard_map/pallas_call | solution.py:332
  21.8 1.5 %collective-permute-done.3.side_ref = f32[256,128]{1,0:T(8,128)S(1)} collective-permute-done((f32[256,128]{1,0:T(8,128)S(1)}, f32[256,128]{1,0:T(8,128)S(1)}, u32[]{:S(2)}, u32[]{:S(2)}) %collective-permute-start.3) | collective-permute-done | bytes 131104 | tf_op jit(solution)/shard_map/ppermute | solution.py:384
  23.3 0.1 shard_map.46.acc_ref
  23.3 0.0 collective-permute-done.4.mate_ref
  23.4 1.4 %shard_map.47 = f32[8,16,1024]{2,1,0:T(8,128)} custom-call(f32[1024,128]{1,0:T(8,128)S(1)} %shard_map.46.acc_ref, f32[256,128]{1,0:T(8,128)S(1)} %collective-permute-done.4.mate_ref, bf16[8,512,512]{2,1,0:T(8,128)(2,1)S(1)} %copy-done), custom_call_target="tpu_custom_call" | custom-call | tf_op jit(solution)/shard_map/pallas_call | solution.py:332
Async XLA Ops:
  0.0 7.0 %copy-start = (bf16[8,512,512]{2,1,0:T(8,128)(2,1)S(1)}, bf16[8,512,512]{2,1,0:T(8,128)(2,1)}, u32[]{:S(2)}) copy-start(bf16[8,512,512]{2,1,0:T(8,128)(2,1)} %constant.2.clone.tab_ref) | copy-start | bytes 12582916
  0.0 1.2 %copy-start.1 = (f32[8,16,1024]{2,1,0:T(8,128)S(1)}, f32[8,16,1024]{2,1,0:T(8,128)}, u32[]{:S(2)}) copy-start(f32[8,16,1024]{2,1,0:T(8,128)} %x_ref.3) | copy-start | bytes 1572868
  1.2 5.0 %copy-start.3 = (f32[2,512,81]{1,0,2:T(2,128)S(1)}, f32[2,512,81]{1,0,2:T(2,128)}, u32[]{:S(2)}) copy-start(f32[2,512,81]{1,0,2:T(2,128)} %param.4) | copy-start | bytes 995332
  1.2 5.8 %copy-start.2 = (f32[8,16,1024]{2,1,0:T(8,128)S(1)}, f32[8,16,1024]{2,1,0:T(8,128)}, u32[]{:S(2)}) copy-start(f32[8,16,1024]{2,1,0:T(8,128)} %x_ref.3) | copy-start | bytes 1572868
  1.3 10.9 %collective-permute-start = (f32[64,1024]{1,0:T(8,128)S(1)}, f32[64,1024]{1,0:T(8,128)S(1)}, u32[]{:S(2)}, u32[]{:S(2)}) collective-permute-start(f32[64,1024]{1,0:T(8,128)S(1)} %get-tuple-element.22), channel_id=1, source_target_pairs={{0,32},{32,0},{64,96},{96,64},{128,160},{160,128},{192,224},{224,1... | collective-permute-start | bytes 786440 | tf_op jit(solution)/shard_map/ppermute | solution.py:364
  3.3 8.9 %collective-permute-start.1 = (f32[16,1024]{1,0:T(8,128)S(1)}, f32[16,1024]{1,0:T(8,128)S(1)}, u32[]{:S(2)}, u32[]{:S(2)}) collective-permute-start(f32[16,1024]{1,0:T(8,128)S(1)} %get-tuple-element.23), channel_id=1, source_target_pairs={{0,1},{1,0},{2,3},{3,2},{4,5},{5,4},{6,7},{7,6},{8,9},{9,8},{10,11... | collective-permute-start | bytes 196616 | tf_op jit(solution)/shard_map/ppermute | solution.py:363
  3.6 16.4 %collective-permute-start.2 = (f32[48,1024]{1,0:T(8,128)S(1)}, f32[48,1024]{1,0:T(8,128)S(1)}, u32[]{:S(2)}, u32[]{:S(2)}) collective-permute-start(f32[48,1024]{1,0:T(8,128)S(1)} %get-tuple-element.26), channel_id=1, source_target_pairs={{0,1},{1,0},{2,3},{3,2},{4,5},{5,4},{6,7},{7,6},{8,9},{9,8},{10,11... | collective-permute-start | bytes 589832 | tf_op jit(solution)/shard_map/ppermute | solution.py:365
  13.2 10.1 %collective-permute-start.3 = (f32[256,128]{1,0:T(8,128)S(1)}, f32[256,128]{1,0:T(8,128)S(1)}, u32[]{:S(2)}, u32[]{:S(2)}) collective-permute-start(f32[256,128]{1,0:T(8,128)S(1)} %get-tuple-element.31), channel_id=1, source_target_pairs={{0,32},{1,2},{2,1},{3,4},{4,3},{5,6},{6,5},{7,8},{8,7},{9,10},{10,... | collective-permute-start | bytes 393224 | tf_op jit(solution)/shard_map/ppermute | solution.py:384
  20.9 2.4 %collective-permute-start.4 = (f32[256,128]{1,0:T(8,128)S(1)}, f32[256,128]{1,0:T(8,128)S(1)}, u32[]{:S(2)}, u32[]{:S(2)}) collective-permute-start(f32[256,128]{1,0:T(8,128)S(1)} %get-tuple-element.32), channel_id=1, source_target_pairs={{0,1},{1,0},{2,3},{3,2},{4,5},{5,4},{6,7},{7,6},{8,9},{9,8},{10,11... | collective-permute-start | bytes 393224 | tf_op jit(solution)/shard_map/ppermute | solution.py:388

commit v5 on v4

--- a/solution.py
+++ b/solution.py
@@ -34,7 +34,7 @@
         table = np.concatenate([np.cos(phase), -np.sin(phase)], axis=1)
         out.extend(split_bf16(table))
         transposed.extend(split_bf16(table.T))
-    return np.stack(out + transposed)
+    return np.stack(out), np.stack(transposed)
 
 
 SUBLANE = ((0, 1, 4, 5), (2, 3, 6, 7))
@@ -253,7 +253,7 @@
     filter_own(fr, fs, h_ref, acc_ref, ahead(), TAPS)
 
 
-def near_kernel(acc_in, nr, ns, h_ref, acc_ref):
+def near_kernel(acc_in, nr, ns, h_ref, inverse_ref, acc_ref):
     acc_ref[...] = acc_in[...]
 
     def body(parity):
@@ -323,7 +323,7 @@
         if parity == 0:
             tiles[0] = jnp.where(lane == 0, 0.5 * tiles[0], tiles[0])
         spectrum = jnp.concatenate(tiles, axis=1)
-        parts.append(dot3(spectrum, tab_ref[4 + 2 * parity], tab_ref[5 + 2 * parity]) * (2.0 / NT))
+        parts.append(dot3(spectrum, tab_ref[2 * parity], tab_ref[2 * parity + 1]) * (2.0 / NT))
     out_ref[:, :, :HALF] = (parts[0] + parts[1]).reshape(ROWS, COLS, HALF)
     out_ref[:, :, HALF:] = (parts[0] - parts[1]).reshape(ROWS, COLS, HALF)
 
@@ -355,7 +355,7 @@
 
 def per_device(traces, filters):
     side, far, near, mate = permutations(lax.axis_size("inline"), lax.axis_size("xline"))
-    tab = jnp.asarray(tables())
+    tab, inverse_tab = (jnp.asarray(table) for table in tables())
     taps = jnp.transpose(filters.reshape(2, HALF // 128, 128, TAPS * TAPS), (3, 1, 0, 2)).reshape(-1, 128)
 
     corner, rest, rows = ((HALO * columns, NT) for columns in (HALO, REST, COLS))
@@ -383,12 +383,12 @@
     )
     from_side = lax.ppermute(to_side, AXES, side)
     (acc,) = call(late_kernel, [wide], [], (acc, fr, fs, h), weight=20)
-    (acc,) = call(near_kernel, [wide], [], (acc, nr, ns, h))
+    (acc,) = call(near_kernel, [wide], [], (acc, nr, ns, h, inverse_tab))
     to_mate, rr, rs = call(mate_kernel, [spot, rest_frame, rest_frame], [], (acc, far_rest, tab, h))
     from_mate = lax.ppermute(to_mate, "xline", mate)
     (acc,) = call(inner_kernel, [frame], [], (acc, rr, rs, sr, ss, h), weight=1)
     (acc,) = call(add_kernel, [frame], [], (acc, from_side), weight=1)
-    (out,) = call(inverse_kernel, [(ROWS, COLS, NT)], [frame], (acc, from_mate, tab))
+    (out,) = call(inverse_kernel, [(ROWS, COLS, NT)], [frame], (acc, from_mate, inverse_tab))
     return out
 
 

time: 24.9 us -> 24.8 us (level)
    unnamed x8 -> x10, local copies, waits for them, and re-layouts: 1.2 us -> 1.06 us
where the time goes in v5:
time: 24.8 us; the launch traced here: 24.6 us
  Pallas kernels  11.4 us (46%)
  starting transfers between devices  8.69 us (35%)
  waiting for transfers between devices  3.4 us (14%)
  local copies, waits for them, and re-layouts  1.06 us (4%)
    pallas_call x11, Pallas kernels, call(): pl.pallas_call(kernel, out_shape=[jax.ShapeDtypeStruct(shape, jnp.float32...  11.4 us
    ppermute x1, starting transfers between devices, per_device(): from_side = lax.ppermute(to_side, AXES, side)  3.66 us
    ppermute x1, starting transfers between devices, per_device(): far_rest = lax.ppermute(far_rest, AXES, far)  2.55 us
    ppermute x1, starting transfers between devices, per_device(): near_rows = lax.ppermute(near_rows, 'inline', near)  2 us
    ppermute x1, waiting for transfers between devices, per_device(): far_side = lax.ppermute(far_side, AXES, far)  1.93 us
    ppermute x1, waiting for transfers between devices, per_device(): from_side = lax.ppermute(to_side, AXES, side)  1.46 us
    unnamed x10, local copies, waits for them, and re-layouts  1.06 us
  transfers between devices with their start and end apart: 5, of which 2 were waited for; matrix products, arithmetic and copies ran while one was open for 0% of the time, Pallas kernels for 40%

profile of v5, /device:TPU:30, one launch (start us, length us, event | category | flops | bytes accessed | tf_op | source)
XLA Modules:
  0.0 24.6 jit_solution(2321672058605898884)
XLA Ops:
  0.0 0.0 copy-start.2
  0.0 1.0 %copy-done.2 = f32[8,16,1024]{2,1,0:T(8,128)S(1)} copy-done((f32[8,16,1024]{2,1,0:T(8,128)S(1)}, f32[8,16,1024]{2,1,0:T(8,128)}, u32[]{:S(2)}) %copy-start.2) | copy-done | bytes 524312
  1.0 0.0 copy-start.4
  1.0 0.0 copy-start
  1.0 0.0 copy-start.3
  1.0 0.1 shard_map.50
  1.1 2.0 %collective-permute-start = (f32[64,1024]{1,0:T(8,128)S(1)}, f32[64,1024]{1,0:T(8,128)S(1)}, u32[]{:S(2)}, u32[]{:S(2)}) collective-permute-start(f32[64,1024]{1,0:T(8,128)S(1)} %get-tuple-element.22), channel_id=1, source_target_pairs={{0,32},{32,0},{64,96},{96,64},{128,160},{160,128},{192,224},{224,1... | collective-permute-start | bytes 786440 | tf_op jit(solution)/shard_map/ppermute | solution.py:364
  3.1 0.4 %collective-permute-start.1 = (f32[16,1024]{1,0:T(8,128)S(1)}, f32[16,1024]{1,0:T(8,128)S(1)}, u32[]{:S(2)}, u32[]{:S(2)}) collective-permute-start(f32[16,1024]{1,0:T(8,128)S(1)} %get-tuple-element.23), channel_id=1, source_target_pairs={{0,1},{1,0},{2,3},{3,2},{4,5},{5,4},{6,7},{7,6},{8,9},{9,8},{10,11... | collective-permute-start | bytes 196616 | tf_op jit(solution)/shard_map/ppermute | solution.py:363
  3.5 2.6 %collective-permute-start.2 = (f32[48,1024]{1,0:T(8,128)S(1)}, f32[48,1024]{1,0:T(8,128)S(1)}, u32[]{:S(2)}, u32[]{:S(2)}) collective-permute-start(f32[48,1024]{1,0:T(8,128)S(1)} %get-tuple-element.26), channel_id=1, source_target_pairs={{0,1},{1,0},{2,3},{3,2},{4,5},{5,4},{6,7},{7,6},{8,9},{9,8},{10,11... | collective-permute-start | bytes 589832 | tf_op jit(solution)/shard_map/ppermute | solution.py:365
  6.0 0.0 copy-done.4
  6.0 0.8 %shard_map.46.h_ref = f32[1296,128]{1,0:T(8,128)S(1)} custom-call(f32[648,128]{1,0:T(8,128)S(1)} %bitcast.5), custom_call_target="tpu_custom_call" | custom-call | tf_op jit(solution)/shard_map/pallas_call | solution.py:332
  6.9 0.0 copy-done
  6.9 0.0 copy-done.3
  6.9 1.5 %shard_map.47 = (f32[1024,128]{1,0:T(8,128)S(1)}, f32[1024,128]{1,0:T(8,128)S(1)}, f32[256,128]{1,0:T(8,128)S(1)}) custom-call(f32[8,16,1024]{2,1,0:T(8,128)S(1)} %copy-done.3, bf16[4,512,512]{2,1,0:T(8,128)(2,1)S(1)} %copy-done, f32[1296,128]{1,0:T(8,128)S(1)} %shard_map.46.h_ref), custom_call_target="tpu_custom_call" | custom-call | tf_op jit(solution)/shard_map/pallas_call | solution.py:332
  8.3 1.8 %shard_map.48.acc_in.acc_ref = f32[1536,128]{1,0:T(8,128)S(1)} custom-call(f32[1024,128]{1,0:T(8,128)S(1)} %get-tuple-element.19.fr, f32[1024,128]{1,0:T(8,128)S(1)} %get-tuple-element.20.fs, f32[1296,128]{1,0:T(8,128)S(1)} %shard_map.46.h_ref), custom_call_target="tpu_custom_call" | custom-call | tf_op jit(solution)/shard_map/pallas_call | solution.py:332
  10.1 1.9 %collective-permute-done.1.far_ref = f32[16,1024]{1,0:T(8,128)S(1)} collective-permute-done((f32[16,1024]{1,0:T(8,128)S(1)}, f32[16,1024]{1,0:T(8,128)S(1)}, u32[]{:S(2)}, u32[]{:S(2)}) %collective-permute-start.1) | collective-permute-done | bytes 65568 | tf_op jit(solution)/shard_map/ppermute | solution.py:363
  12.0 0.0 collective-permute-done.near_ref
  12.0 1.0 %shard_map.51 = (f32[256,128]{1,0:T(8,128)S(1)}, f32[512,128]{1,0:T(8,128)S(1)}, f32[512,128]{1,0:T(8,128)S(1)}, f32[128,128]{1,0:T(8,128)S(1)}, f32[128,128]{1,0:T(8,128)S(1)}) custom-call(f32[256,128]{1,0:T(8,128)S(1)} %get-tuple-element.21.own_ref, f32[64,1024]{1,0:T(8,128)S(1)} %collective-permute-done.near_ref, ...), custom_call_target="tpu_custom_call" | custom-call | tf_op jit(solution)/shard_map/pallas_call | solution.py:332
  13.0 0.0 copy-start.1
  13.1 3.7 %collective-permute-start.3 = (f32[256,128]{1,0:T(8,128)S(1)}, f32[256,128]{1,0:T(8,128)S(1)}, u32[]{:S(2)}, u32[]{:S(2)}) collective-permute-start(f32[256,128]{1,0:T(8,128)S(1)} %get-tuple-element.31), channel_id=1, source_target_pairs={{0,32},{1,2},{2,1},{3,4},{4,3},{5,6},{6,5},{7,8},{8,7},{9,10},{10,... | collective-permute-start | bytes 393224 | tf_op jit(solution)/shard_map/ppermute | solution.py:384
  16.7 2.4 %shard_map.49.acc_in = f32[1536,128]{1,0:T(8,128)S(1)} custom-call(f32[1536,128]{1,0:T(8,128)S(1)} %shard_map.48.acc_in.acc_ref, f32[1024,128]{1,0:T(8,128)S(1)} %get-tuple-element.19.fr, f32[1024,128]{1,0:T(8,128)S(1)} %get-tuple-element.20.fs, f32[1296,128]{1,0:T(8,128)S(1)} %shard_map.46.h_ref), custom_call_target="tpu_custom_call" | custom-call | flops 20000000000 | tf_op jit(solution)/shard_map/pallas_call | solution.py:332
  19.1 0.0 copy-done.1
  19.1 0.8 %shard_map.52.acc_ref = f32[1536,128]{1,0:T(8,128)S(1)} custom-call(f32[1536,128]{1,0:T(8,128)S(1)} %shard_map.49.acc_in, f32[512,128]{1,0:T(8,128)S(1)} %get-tuple-element.24.nr, f32[512,128]{1,0:T(8,128)S(1)} %get-tuple-element.25.ns, f32[1296,128]{1,0:T(8,128)S(1)} %shard_map.46.h_ref, bf16[4,512,512]{2,1,0:T(8,128)(2,1)S(1)} %copy-done.1), custom_call_target="tpu_custom_call" | custom-call | tf_op jit(solution)/shard_map/pallas_call | solution.py:332
  19.9 0.0 collective-permute-done.2.rest_ref
  20.0 0.8 %shard_map.53 = (f32[256,128]{1,0:T(8,128)S(1)}, f32[384,128]{1,0:T(8,128)S(1)}, f32[384,128]{1,0:T(8,128)S(1)}) custom-call(f32[1536,128]{1,0:T(8,128)S(1)} %shard_map.52.acc_ref, f32[48,1024]{1,0:T(8,128)S(1)} %collective-permute-done.2.rest_ref, bf16[4,512,512]{2,1,0:T(8,128)(2,1)S(1)} %copy-done, f32[1296,128]{1,0:T(8,128)S(1)} %shard_map.46.h_ref), custom_call_target="tpu_custom_call" | custom-call | tf_op jit(solution)/shard_map/pallas_call | solution.py:332
  20.8 0.1 collective-permute-start.4
  20.9 0.8 %shard_map.54.acc_ref = f32[1024,128]{1,0:T(8,128)S(1)} custom-call(f32[1536,128]{1,0:T(8,128)S(1)} %shard_map.52.acc_ref, f32[384,128]{1,0:T(8,128)S(1)} %get-tuple-element.27.rr, f32[384,128]{1,0:T(8,128)S(1)} %get-tuple-element.28.rs, f32[128,128]{1,0:T(8,128)S(1)} %get-tuple-element.29.sr, f32[128,128]{1,0:T(8,128)S(1)} %get-tuple-element.30.ss, ...), custom_call_target="tpu_custom_call" | custom-call | flops 1000000000 | tf_op jit(solution)/shard_map/pallas_call | solution.py:332
  21.7 1.5 %collective-permute-done.3.side_ref = f32[256,128]{1,0:T(8,128)S(1)} collective-permute-done((f32[256,128]{1,0:T(8,128)S(1)}, f32[256,128]{1,0:T(8,128)S(1)}, u32[]{:S(2)}, u32[]{:S(2)}) %collective-permute-start.3) | collective-permute-done | bytes 131104 | tf_op jit(solution)/shard_map/ppermute | solution.py:384
  23.1 0.1 shard_map.55.acc_ref
  23.2 0.0 collective-permute-done.4.mate_ref
  23.2 1.4 %shard_map.56 = f32[8,16,1024]{2,1,0:T(8,128)} custom-call(f32[1024,128]{1,0:T(8,128)S(1)} %shard_map.55.acc_ref, f32[256,128]{1,0:T(8,128)S(1)} %collective-permute-done.4.mate_ref, bf16[4,512,512]{2,1,0:T(8,128)(2,1)S(1)} %copy-done.1), custom_call_target="tpu_custom_call" | custom-call | tf_op jit(solution)/shard_map/pallas_call | solution.py:332
Async XLA Ops:
  0.0 1.0 %copy-start.2 = (f32[8,16,1024]{2,1,0:T(8,128)S(1)}, f32[8,16,1024]{2,1,0:T(8,128)}, u32[]{:S(2)}) copy-start(f32[8,16,1024]{2,1,0:T(8,128)} %x_ref.3) | copy-start | bytes 1572868
  1.0 5.0 %copy-start.4 = (f32[2,512,81]{1,0,2:T(2,128)S(1)}, f32[2,512,81]{1,0,2:T(2,128)}, u32[]{:S(2)}) copy-start(f32[2,512,81]{1,0,2:T(2,128)} %param.5) | copy-start | bytes 995332
  1.0 5.8 %copy-start = (bf16[4,512,512]{2,1,0:T(8,128)(2,1)S(1)}, bf16[4,512,512]{2,1,0:T(8,128)(2,1)}, u32[]{:S(2)}) copy-start(bf16[4,512,512]{2,1,0:T(8,128)(2,1)} %constant.4.clone.tab_ref) | copy-start | bytes 6291460
  1.0 5.8 %copy-start.3 = (f32[8,16,1024]{2,1,0:T(8,128)S(1)}, f32[8,16,1024]{2,1,0:T(8,128)}, u32[]{:S(2)}) copy-start(f32[8,16,1024]{2,1,0:T(8,128)} %x_ref.3) | copy-start | bytes 1572868
  1.1 10.9 %collective-permute-start = (f32[64,1024]{1,0:T(8,128)S(1)}, f32[64,1024]{1,0:T(8,128)S(1)}, u32[]{:S(2)}, u32[]{:S(2)}) collective-permute-start(f32[64,1024]{1,0:T(8,128)S(1)} %get-tuple-element.22), channel_id=1, source_target_pairs={{0,32},{32,0},{64,96},{96,64},{128,160},{160,128},{192,224},{224,1... | collective-permute-start | bytes 786440 | tf_op jit(solution)/shard_map/ppermute | solution.py:364
  3.1 8.9 %collective-permute-start.1 = (f32[16,1024]{1,0:T(8,128)S(1)}, f32[16,1024]{1,0:T(8,128)S(1)}, u32[]{:S(2)}, u32[]{:S(2)}) collective-permute-start(f32[16,1024]{1,0:T(8,128)S(1)} %get-tuple-element.23), channel_id=1, source_target_pairs={{0,1},{1,0},{2,3},{3,2},{4,5},{5,4},{6,7},{7,6},{8,9},{9,8},{10,11... | collective-permute-start | bytes 196616 | tf_op jit(solution)/shard_map/ppermute | solution.py:363
  3.5 16.5 %collective-permute-start.2 = (f32[48,1024]{1,0:T(8,128)S(1)}, f32[48,1024]{1,0:T(8,128)S(1)}, u32[]{:S(2)}, u32[]{:S(2)}) collective-permute-start(f32[48,1024]{1,0:T(8,128)S(1)} %get-tuple-element.26), channel_id=1, source_target_pairs={{0,1},{1,0},{2,3},{3,2},{4,5},{5,4},{6,7},{7,6},{8,9},{9,8},{10,11... | collective-permute-start | bytes 589832 | tf_op jit(solution)/shard_map/ppermute | solution.py:365
  13.0 6.1 %copy-start.1 = (bf16[4,512,512]{2,1,0:T(8,128)(2,1)S(1)}, bf16[4,512,512]{2,1,0:T(8,128)(2,1)}, u32[]{:S(2)}) copy-start(bf16[4,512,512]{2,1,0:T(8,128)(2,1)} %constant.5.clone.inverse_ref.tab_ref) | copy-start | bytes 6291460
  13.1 10.1 %collective-permute-start.3 = (f32[256,128]{1,0:T(8,128)S(1)}, f32[256,128]{1,0:T(8,128)S(1)}, u32[]{:S(2)}, u32[]{:S(2)}) collective-permute-start(f32[256,128]{1,0:T(8,128)S(1)} %get-tuple-element.31), channel_id=1, source_target_pairs={{0,32},{1,2},{2,1},{3,4},{4,3},{5,6},{6,5},{7,8},{8,7},{9,10},{10,... | collective-permute-start | bytes 393224 | tf_op jit(solution)/shard_map/ppermute | solution.py:384
  20.8 2.4 %collective-permute-start.4 = (f32[256,128]{1,0:T(8,128)S(1)}, f32[256,128]{1,0:T(8,128)S(1)}, u32[]{:S(2)}, u32[]{:S(2)}) collective-permute-start(f32[256,128]{1,0:T(8,128)S(1)} %get-tuple-element.32), channel_id=1, source_target_pairs={{0,1},{1,0},{2,3},{3,2},{4,5},{5,4},{6,7},{7,6},{8,9},{9,8},{10,11... | collective-permute-start | bytes 393224 | tf_op jit(solution)/shard_map/ppermute | solution.py:388
